TPU v7x, 32 devices: a whole 2x2x4 slice. The times are simulated.
32 devices in a mesh: shard: 4 (over y, core), replica: 8 (over z, x).
Axes of the slice: x: 2, y: 2, z: 4, core: 2. Of those that a mesh axis runs over, the one named last changes fastest.
Arguments:
- tokens: bfloat16 [64, 256, 384], P(('shard', 'replica')), may hold values from -6 to 6
- condition: bfloat16 [64, 384], P(('shard', 'replica')), may hold values from -6 to 6
- cotangent: bfloat16 [64, 256, 384], P(('shard', 'replica')), may hold values from -6 to 6
- w_rows: bfloat16 [384, 5376], P('shard'), may hold values from -1.2247449 to 1.2247449
- w_down: bfloat16 [1536, 384], P('shard'), may hold values from -0.15625 to 0.15625
- bias_pack: bfloat16 [5376], P('shard'), may hold values from -1 to 1
- rows_first: bfloat16 [384, 5376], P('shard'), may hold values from -40.96 to 40.96
- rows_second: bfloat16 [384, 5376], P('shard'), may hold values from 0.32768 to 32.768
- down_first: bfloat16 [1536, 384], P('shard'), may hold values from -16.625 to 16.625
- down_second: bfloat16 [1536, 384], P('shard'), may hold values from 1.46875 to 5.875
- bias_first: bfloat16 [5376], P('shard'), may hold values from -69.12 to 69.12
- bias_second: bfloat16 [5376], P('shard'), may hold values from 0.32768 to 95.0272
Outputs:
- block_out: bfloat16 [64, 256, 384], P(('shard', 'replica'))
- tokens_grad: bfloat16 [64, 256, 384], P(('shard', 'replica'))
- cond_grad: float32 [64, 384], P(('shard', 'replica'))
- rows_new: float32 [384, 5376], P('shard')
- rows_first_new: float32 [384, 5376], P('shard')
- rows_second_new: float32 [384, 5376], P('shard')
- down_new: float32 [1536, 384], P('shard')
- down_first_new: float32 [1536, 384], P('shard')
- down_second_new: float32 [1536, 384], P('shard')
- bias_new: float32 [5376], P('shard')
- bias_first_new: float32 [5376], P('shard')
- bias_second_new: float32 [5376], P('shard')
All inputs are finite; a program needn't handle non-finite values.
Results may differ from a plain program's by a relative error of at most 0.012.
The roundings to bfloat16 on the way count: a program that leaves them out, or rounds other values in their place, can miss the bound.
Values may be sent and summed in bfloat16 or wider, within the bound.
A program may use at most 128 MiB of HBM per device.

v0:
```python
from functools import partial

import jax
import jax.numpy as jnp
from jax import lax
from jax.sharding import PartitionSpec as P

HEADS = 6
HEAD = 64
STEP = 10


norm_eps = 1e-06
beta_one = 0.9
beta_two = 0.999
adam_eps = 1e-08
decay_rate = 0.1
learn_rate = 0.1


def normalize(values):
    average = jnp.mean(values, axis=-1, keepdims=True)
    centered = values - average
    variance = jnp.mean(centered * centered, axis=-1, keepdims=True)
    inv_std = lax.rsqrt(variance + norm_eps)
    return (centered * inv_std, inv_std)


def norm_back(gradient, normed, inv_std):
    return inv_std * (
        gradient
        - jnp.mean(gradient, axis=-1, keepdims=True)
        - normed * jnp.mean(gradient * normed, axis=-1, keepdims=True)
    )


def matrix_multiply(spec_text, left, right):
    return jnp.einsum(spec_text, left, right, preferred_element_type=jnp.float32)


def adam_step(weight, gradient, moment_one, moment_two, weight_decay):
    first_new = beta_one * moment_one.astype(jnp.float32) + (1.0 - beta_one) * gradient
    second_new = beta_two * moment_two.astype(jnp.float32) + (1.0 - beta_two) * gradient * gradient
    first_hat = first_new / (1.0 - beta_one**STEP)
    second_hat = second_new / (1.0 - beta_two**STEP)
    master = weight.astype(jnp.float32)
    updated = master - learn_rate * (
        first_hat / (jnp.sqrt(second_hat) + adam_eps) + weight_decay * master
    )
    return (updated, first_new, second_new)


def per_device(
    tokens,
    condition,
    cotangent,
    w_rows,
    w_down,
    bias_pack,
    rows_first,
    rows_second,
    down_first,
    down_second,
    bias_first,
    bias_second,
):
    latents, positions, embedding_width = tokens.shape
    hidden_units_width = w_rows.shape[1] - 10 * embedding_width
    six_width = 6 * embedding_width
    cond_matrix, bias_full = (
        lax.all_gather(w_rows[:, :six_width], "shard", axis=0, tiled=True),
        lax.all_gather(bias_pack, "shard", axis=0, tiled=True),
    )
    bias_entries = bias_full.astype(jnp.float32)
    cond_values = condition.astype(jnp.float32)
    silu_cond = jax.nn.silu(cond_values).astype(jnp.bfloat16)
    modulation = matrix_multiply("ld,de->le", silu_cond, cond_matrix) + bias_entries[:six_width]
    blocks_six = [
        modulation[:, None, index * embedding_width : (index + 1) * embedding_width]
        for index in range(6)
    ]
    shift_attention, scale_attention, gate_attention, shift_feed, scale_feed, gate_feed = blocks_six
    triple_matrix, output_matrix = (
        lax.all_gather(w_rows[:, six_width : 9 * embedding_width], "shard", axis=0, tiled=True),
        lax.all_gather(
            w_rows[:, 9 * embedding_width : 10 * embedding_width], "shard", axis=0, tiled=True
        ),
    )
    token_values = tokens.astype(jnp.float32)
    normed_attention, inv_attention = normalize(token_values)
    input_attention = (normed_attention * (1.0 + scale_attention) + shift_attention).astype(
        jnp.bfloat16
    )
    zeros_key = jnp.zeros((embedding_width,), jnp.float32)
    triple_bias = jnp.concatenate(
        [
            bias_entries[six_width : 7 * embedding_width],
            zeros_key,
            bias_entries[7 * embedding_width : 8 * embedding_width],
        ]
    )
    projected = (
        matrix_multiply("lsd,de->lse", input_attention, triple_matrix) + triple_bias
    ).astype(jnp.bfloat16)
    head_shape = (latents, positions, HEADS, HEAD)
    flat_shape = (latents, positions, embedding_width)
    query = projected[..., :embedding_width].reshape(head_shape)
    keys = projected[..., embedding_width : 2 * embedding_width].reshape(head_shape)
    values = projected[..., 2 * embedding_width :].reshape(head_shape)
    score_scale = HEAD ** (-0.5)
    scores = matrix_multiply("lqhe,lkhe->lhqk", query, keys) * score_scale
    log_total = jax.nn.logsumexp(scores, axis=-1, keepdims=True)
    softmax_low = jnp.exp(scores - log_total).astype(jnp.bfloat16)
    mixed_heads = (
        matrix_multiply("lhqk,lkhe->lqhe", softmax_low, values)
        .reshape(flat_shape)
        .astype(jnp.bfloat16)
    )
    branch = (
        matrix_multiply("lsd,de->lse", mixed_heads, output_matrix)
        + bias_entries[8 * embedding_width : 9 * embedding_width]
    )
    residual = token_values + gate_attention * branch
    normed_feed, inv_feed = normalize(residual)
    feed_input = (normed_feed * (1.0 + scale_feed) + shift_feed).astype(jnp.bfloat16)
    expand_weight, shrink_weight = (
        lax.all_gather(w_rows[:, 10 * embedding_width :], "shard", axis=0, tiled=True),
        lax.all_gather(w_down, "shard", axis=0, tiled=True),
    )
    hidden = (
        matrix_multiply("wqg,gc->wqc", feed_input, expand_weight)
        + bias_entries[9 * embedding_width : 9 * embedding_width + hidden_units_width]
    )
    gelu_out, gelu_pull = jax.vjp(partial(jax.nn.gelu, approximate=True), hidden)
    activated_hidden = gelu_out.astype(jnp.bfloat16)
    feed_out = (
        matrix_multiply("wku,ux->wkx", activated_hidden, shrink_weight)
        + bias_entries[9 * embedding_width + hidden_units_width :]
    )
    block_out = (residual + gate_feed * feed_out).astype(jnp.bfloat16)
    rows_whole, shrink_weight = (
        lax.all_gather(w_rows, "shard", axis=0, tiled=True),
        lax.all_gather(w_down, "shard", axis=0, tiled=True),
    )
    cond_matrix = rows_whole[:, :six_width]
    triple_matrix = rows_whole[:, six_width : 9 * embedding_width]
    output_matrix = rows_whole[:, 9 * embedding_width : 10 * embedding_width]
    expand_weight = rows_whole[:, 10 * embedding_width :]
    upstream = cotangent.astype(jnp.float32)
    delta_gate_feed = jnp.sum(upstream * feed_out, axis=1)
    delta_feed_branch = (gate_feed * upstream).astype(jnp.bfloat16)
    summed_down_weight = matrix_multiply("pxz,pxk->zk", activated_hidden, delta_feed_branch)
    bias_down = jnp.sum(delta_feed_branch.astype(jnp.float32), axis=(0, 1))
    delta_activated = matrix_multiply("tgw,uw->tgu", delta_feed_branch, shrink_weight)
    delta_hidden_units = gelu_pull(delta_activated)[0].astype(jnp.bfloat16)
    summed_expand_weight = matrix_multiply("pce,pcw->ew", feed_input, delta_hidden_units)
    bias_expand = jnp.sum(delta_hidden_units.astype(jnp.float32), axis=(0, 1))
    delta_feed_input = matrix_multiply("kzq,wq->kzw", delta_hidden_units, expand_weight)
    delta_shift_feed = jnp.sum(delta_feed_input, axis=1)
    delta_scale_feed = jnp.sum(delta_feed_input * normed_feed, axis=1)
    delta_residual = upstream + norm_back(
        delta_feed_input * (1.0 + scale_feed), normed_feed, inv_feed
    )
    delta_gate_attention = jnp.sum(delta_residual * branch, axis=1)
    delta_branch = (gate_attention * delta_residual).astype(jnp.bfloat16)
    total_output = matrix_multiply("lsd,lse->de", mixed_heads, delta_branch)
    bias_output = jnp.sum(delta_branch.astype(jnp.float32), axis=(0, 1))
    delta_mixed = (
        matrix_multiply("lse,de->lsd", delta_branch, output_matrix)
        .astype(jnp.bfloat16)
        .reshape(head_shape)
    )
    scores_again = matrix_multiply("lqhe,lkhe->lhqk", query, keys) * score_scale
    softmax_full = jnp.exp(scores_again - log_total)
    softmax_again = softmax_full.astype(jnp.bfloat16)
    delta_soft = matrix_multiply("lqhe,lkhe->lhqk", delta_mixed, values)
    delta_values = matrix_multiply("lhqk,lqhe->lkhe", softmax_again, delta_mixed).astype(
        jnp.bfloat16
    )
    row_inner = jnp.sum(delta_soft * softmax_full, axis=-1, keepdims=True)
    delta_scores = (softmax_full * (delta_soft - row_inner)).astype(jnp.bfloat16)
    delta_query = (matrix_multiply("lhqk,lkhe->lqhe", delta_scores, keys) * score_scale).astype(
        jnp.bfloat16
    )
    delta_keys = (matrix_multiply("lhqk,lqhe->lkhe", delta_scores, query) * score_scale).astype(
        jnp.bfloat16
    )
    delta_projected = jnp.concatenate(
        [
            delta_query.reshape(flat_shape),
            delta_keys.reshape(flat_shape),
            delta_values.reshape(flat_shape),
        ],
        axis=-1,
    )
    total_triple = matrix_multiply("lsd,lse->de", input_attention, delta_projected)
    bias_query = jnp.sum(delta_query.reshape(flat_shape).astype(jnp.float32), axis=(0, 1))
    bias_valued = jnp.sum(delta_values.reshape(flat_shape).astype(jnp.float32), axis=(0, 1))
    delta_input_attention = matrix_multiply("lse,de->lsd", delta_projected, triple_matrix)
    delta_shift_attention = jnp.sum(delta_input_attention, axis=1)
    delta_scale_attention = jnp.sum(delta_input_attention * normed_attention, axis=1)
    delta_tokens = delta_residual + norm_back(
        delta_input_attention * (1.0 + scale_attention), normed_attention, inv_attention
    )
    tokens_grad = delta_tokens.astype(jnp.bfloat16)
    delta_modulation = jnp.concatenate(
        [
            delta_shift_attention,
            delta_scale_attention,
            delta_gate_attention,
            delta_shift_feed,
            delta_scale_feed,
            delta_gate_feed,
        ],
        axis=1,
    ).astype(jnp.bfloat16)
    total_cond = matrix_multiply("ld,le->de", silu_cond, delta_modulation)
    bias_cond = jnp.sum(delta_modulation.astype(jnp.float32), axis=0)
    delta_silu = matrix_multiply("le,de->ld", delta_modulation, cond_matrix)
    cond_grad = jax.vjp(jax.nn.silu, cond_values)[1](delta_silu)[0]
    total_bias = jnp.concatenate(
        [bias_cond, bias_query, bias_valued, bias_output, bias_expand, bias_down]
    )
    total_rows = jnp.concatenate(
        [total_cond, total_triple, total_output, summed_expand_weight], axis=1
    )
    rows_share, down_share, bias_share = (
        lax.psum_scatter(total_rows, "shard", scatter_dimension=0, tiled=True),
        lax.psum_scatter(summed_down_weight, "shard", scatter_dimension=0, tiled=True),
        lax.psum_scatter(total_bias, "shard", scatter_dimension=0, tiled=True),
    )
    rows_grad, down_grad, bias_grad = lax.psum((rows_share, down_share, bias_share), "replica")
    rows_new, rows_first_new, rows_second_new = adam_step(
        w_rows, rows_grad, rows_first, rows_second, decay_rate
    )
    down_new, down_first_new, down_second_new = adam_step(
        w_down, down_grad, down_first, down_second, decay_rate
    )
    bias_new, bias_first_new, bias_second_new = adam_step(
        bias_pack, bias_grad, bias_first, bias_second, 0.0
    )
    return (
        block_out,
        tokens_grad,
        cond_grad,
        rows_new,
        rows_first_new,
        rows_second_new,
        down_new,
        down_first_new,
        down_second_new,
        bias_new,
        bias_first_new,
        bias_second_new,
    )


def solution(mesh):
    placed = (
        P(("shard", "replica"), None, None),
        P(("shard", "replica"), None),
        P(("shard", "replica"), None, None),
        P("shard", None),
        P("shard", None),
        P("shard"),
        P("shard", None),
        P("shard", None),
        P("shard", None),
        P("shard", None),
        P("shard"),
        P("shard"),
    )
    return jax.shard_map(
        per_device,
        mesh=mesh,
        in_specs=placed,
        out_specs=(
            P(("shard", "replica"), None, None),
            P(("shard", "replica"), None, None),
            P(("shard", "replica"), None),
            P("shard", None),
            P("shard", None),
            P("shard", None),
            P("shard", None),
            P("shard", None),
            P("shard", None),
            P("shard"),
            P("shard"),
            P("shard"),
        ),
        check_vma=False,
    )
```

profile of v0, /device:TPU:0, one launch (start us, length us, event | category | flops | bytes accessed | tf_op | source)
XLA Modules:
  0.0 353.5 jit_solution(4771571126846170216)
XLA Ops:
  13.9 13.2 %all-reduce = bf16[5376]{0:T(1024)(128)(2,1)S(1)} all-reduce(bf16[5376]{0:T(1024)(128)(2,1)S(1)} %dynamic-update-slice), channel_id=1, replica_groups=mesh['shard'=4,'replica'=8] {'shard'}, use_global_device_ids=true, to_apply=%add | all-reduce | flops 5376 | bytes 21504
  30.1 6.3 %all_gather.25 = bf16[384,384]{1,0:T(8,128)(2,1)} all-gather(bf16[96,384]{1,0:T(8,128)(2,1)S(1)} %slice.80), channel_id=1, replica_groups=mesh['shard'=4,'replica'=8] {'shard'}, dimensions={0}, use_global_device_ids=true | all-gather | bytes 368640 | tf_op jit(solution)/shard_map/all_gather | solution.py:85
  36.9 9.3 %all_gather.24 = bf16[384,1152]{1,0:T(8,128)(2,1)S(1)} all-gather(bf16[96,1152]{1,0:T(8,128)(2,1)S(1)} %slice.74), channel_id=1, replica_groups=mesh['shard'=4,'replica'=8] {'shard'}, dimensions={0}, use_global_device_ids=true | all-gather | bytes 1105920 | tf_op jit(solution)/shard_map/all_gather | solution.py:84
  60.0 4.3 %convolution_add_fusion.1 = f32[2,256,1536]{2,1,0:T(8,128)} fusion(f32[1536]{0:T(1024)} %slice.105, bf16[384,1536]{1,0:T(8,128)(2,1)} %all-gather.7.cloned.1.call-done, f32[2,256,384]{2,1,0:T(8,128)} %copy-done.8, f32[2,384]{1,0:T(2,128)} %get-tuple-element.48, f32[2,384]{1,0:T(2,128)} %get-tuple-element.49, f32[2,256]{1,0:T(2,128)} %add_rsqrt_fusion, ...), kind=kOutput, calls=%fused_computation.4 | convolution fusion | flops 605749248 | bytes 5128192 | tf_op jit(solution)/shard_map/wqg,gc->wqc/dot_general | solution.py:38
  64.3 8.2 %all-gather.9.cloned.1.call-done = bf16[1536,384]{1,0:T(8,128)(2,1)} async-done(((bf16[384,384]{1,0:T(8,128)(2,1)}), bf16[1536,384]{1,0:T(8,128)(2,1)}) %all-gather.9.cloned.1.call-update) | async-done | bytes 1179664 | tf_op jit(solution)/shard_map/all_gather | solution.py:128
  72.5 5.7 %convert_reduce_fusion = (f32[1536]{0:T(1024)}, bf16[2,256,1536]{2,1,0:T(8,128)(2,1)S(1)}) fusion(f32[2,256,1536]{2,1,0:T(8,128)} %convolution_add_fusion.1, bf16[1536,384]{1,0:T(8,128)(2,1)} %all-gather.9.cloned.1.call-done, bf16[2,256,384]{2,1,0:T(8,128)(2,1)} %param.14, f32[2,384]{1,0:T(2,128)} %get-tuple-element.47), kind=kOutput, calls=%fused_computation.13 | convolution fusion | flops 621869568 | bytes 6300672 | tf_op jit(solution)/shard_map/tgw,uw->tgu/dot_general | solution.py:38
  78.2 2.4 convolution_bitcast_fusion.1
  81.9 2.8 convolution_bitcast_fusion
  85.0 23.1 %all-gather.11.cloned.1.call-done = bf16[384,5376]{1,0:T(8,128)(2,1)} async-done(((bf16[96,5376]{1,0:T(8,128)(2,1)}), bf16[384,5376]{1,0:T(8,128)(2,1)}) %all-gather.11.cloned.1.call-update) | async-done | bytes 4128784 | tf_op jit(solution)/shard_map/all_gather | solution.py:142
  108.1 3.9 %multiply_reduce_fusion.2 = (bf16[2,384]{1,0:T(2,128)(2,1)}, f32[2,256]{1,0:T(2,128)S(1)}, f32[2,256]{1,0:T(2,128)S(1)}, bf16[2,384]{1,0:T(2,128)(2,1)}, f32[2,256,384]{2,1,0:T(8,128)S(1)}) fusion(f32[2,256,384]{2,1,0:T(8,128)} %copy-done.8, f32[2,256]{1,0:T(2,128)} %add_rsqrt_fusion, f32[2,256]{1,0:T(2,128)} %copy-done.35, ...), kind=kOutput, calls=%fused_computation.81 | convolution fusion | flops 605746688 | bytes 4339712 | tf_op jit(solution)/shard_map/kzq,wq->kzw/dot_general | solution.py:38
  112.1 3.2 convert_reduce_fusion.2
  116.1 2.1 convolution_convert_fusion.2
  120.2 3.0 convert_reduce_fusion.4
  125.1 2.0 multiply_reduce_fusion
  131.1 2.0 fusion.15
  134.1 2.5 fusion.35
  141.0 3.5 pad_maximum_fusion
  144.7 72.5 %reduce-scatter.3.cloned.1.call-done = f32[96,5376]{1,0:T(8,128)} async-done(((f32[384,5376]{1,0:T(8,128)}), f32[96,5376]{1,0:T(8,128)}) %reduce-scatter.3.cloned.1.call-update) | async-done | bytes 2064400 | tf_op jit(solution)/shard_map/reduce_scatter | solution.py:228
  218.2 10.3 %all-reduce.1 = f32[5376]{0:T(1024)S(1)} all-reduce(f32[5376]{0:T(1024)S(1)} %constant_dynamic-update-slice_fusion.7), channel_id=4, replica_groups=mesh['shard'=4,'replica'=8] {'shard'}, use_global_device_ids=true, to_apply=%region_27.28.clone | all-reduce | flops 5376 | bytes 43008
  228.5 23.4 %psum.23 = f32[1344]{0:T(1024)S(1)} all-reduce(f32[1344]{0:T(1024)S(1)} %dynamic-slice.2), channel_id=1, replica_groups=mesh['shard'=4,'replica'=8] {'replica'}, use_global_device_ids=true, to_apply=%region_28.29 | all-reduce | flops 1344 | bytes 10752 | tf_op jit(solution)/shard_map/psum | solution.py:232
  252.5 2.7 fusion.57
  255.2 83.2 %all-reduce.5.cloned.1.call-done = (f32[96,5376]{1,0:T(8,128)}, f32[384,384]{1,0:T(8,128)}) async-done(((f32[96,5376]{1,0:T(8,128)}, f32[384,384]{1,0:T(8,128)}), (f32[96,5376]{1,0:T(8,128)}, f32[384,384]{1,0:T(8,128)})) %all-reduce.5.cloned.1.call-update) | async-done | bytes 2654224 | tf_op jit(solution)/shard_map/psum | solution.py:232
  338.5 2.9 convert_subtract_fusion.2
  341.4 5.2 %convert_subtract_fusion = (f32[96,5376]{1,0:T(8,128)}, f32[96,5376]{1,0:T(8,128)}, f32[96,5376]{1,0:T(8,128)}) fusion(bf16[96,5376]{1,0:T(8,128)(2,1)S(1)} %copy-done.1, f32[96,5376]{1,0:T(8,128)S(1)} %copy-done.13, bf16[96,5376]{1,0:T(8,128)(2,1)} %param.18, bf16[96,5376]{1,0:T(8,128)(2,1)} %param.19), kind=kLoop, calls=%fused_computation.25 | loop fusion | flops 9289728 | bytes 11354112 | tf_op jit(solution)/shard_map/sub | solution.py:47
  (220 shorter events, 39.5 us)
Async XLA Ops:
  7.2 6.4 %copy-start.28 = (bf16[1344]{0:T(1024)(128)(2,1)S(1)}, bf16[1344]{0:T(1024)(128)(2,1)}, u32[]{:S(2)}) copy-start(bf16[1344]{0:T(1024)(128)(2,1)} %param.17) | copy-start | bytes 8068
  7.2 29.2 %copy-start.2 = (bf16[2,256,384]{2,1,0:T(8,128)(2,1)S(1)}, bf16[2,256,384]{2,1,0:T(8,128)(2,1)}, u32[]{:S(2)}) copy-start(bf16[2,256,384]{2,1,0:T(8,128)(2,1)} %param.12) | copy-start | bytes 1179652
  7.2 38.9 %copy-start.43 = (bf16[2,384]{1,0:T(2,128)(2,1)S(1)}, bf16[2,384]{1,0:T(2,128)(2,1)}, u32[]{:S(2)}) copy-start(bf16[2,384]{1,0:T(2,128)(2,1)} %param.13) | copy-start | bytes 4612
  7.2 38.9 %all-gather.5.cloned.1.call-start = ((), (), s32[]{:S(2)}) async-start(), calls=%async_computation.2 | async-start | bytes 2211840 | tf_op jit(solution)/shard_map/all_gather | solution.py:71
  9.1 50.9 %all-gather.7.cloned.1.call-start = ((), (), s32[]{:S(2)}) async-start(), calls=%async_computation.3 | async-start | bytes 1474560 | tf_op jit(solution)/shard_map/all_gather | solution.py:127
  10.9 61.6 %all-gather.9.cloned.1.call-start = ((), (), s32[]{:S(2)}) async-start(), calls=%async_computation.4 | async-start | bytes 1474560 | tf_op jit(solution)/shard_map/all_gather | solution.py:128
  11.7 96.4 %all-gather.11.cloned.1.call-start = ((), (), s32[]{:S(2)}) async-start(), calls=%async_computation.5 | async-start | bytes 5160960 | tf_op jit(solution)/shard_map/all_gather | solution.py:142
  12.2 132.4 %reduce-scatter.5.cloned.1.call-start = ((), (), s32[]{:S(2)}) async-start(), calls=%async_computation.7 | async-start | bytes 2949120 | tf_op jit(solution)/shard_map/reduce_scatter | solution.py:229
  36.6 12.0 %copy-start.24 = (f32[2,256]{1,0:T(2,128)}, f32[2,256]{1,0:T(2,128)S(1)}, u32[]{:S(2)}) copy-start(f32[2,256]{1,0:T(2,128)S(1)} %broadcast_multiply_fusion.5) | copy-start | bytes 6148
  36.9 11.7 %copy-start.39 = (f32[2,256]{1,0:T(2,128)}, f32[2,256]{1,0:T(2,128)S(1)}, u32[]{:S(2)}) copy-start(f32[2,256]{1,0:T(2,128)S(1)} %add_rsqrt_fusion.1) | copy-start | bytes 6148
  72.5 5.7 %copy-start.58 = (f32[2,256]{1,0:T(2,128)S(1)}, f32[2,256]{1,0:T(2,128)}, u32[]{:S(2)}) copy-start(f32[2,256]{1,0:T(2,128)} %add_rsqrt_fusion) | copy-start | bytes 6148
  84.7 132.4 %reduce-scatter.3.cloned.1.call-start = ((), (), s32[]{:S(2)}) async-start(), calls=%async_computation.6 | async-start | bytes 10321920 | tf_op jit(solution)/shard_map/reduce_scatter | solution.py:228
  144.5 73.4 %copy-start.26 = (f32[6,64]{1,0:T(8,128)S(1)}, f32[6,64]{1,0:T(8,128)}, u32[]{:S(2)}) copy-start(f32[6,64]{1,0:T(8,128)} %get-tuple-element.68) | copy-start | bytes 4612
  144.5 73.5 %copy-start.27 = (f32[6,64]{1,0:T(8,128)S(1)}, f32[6,64]{1,0:T(8,128)}, u32[]{:S(2)}) copy-start(f32[6,64]{1,0:T(8,128)} %get-tuple-element.66) | copy-start | bytes 4612
  144.5 73.6 %copy-start.57 = (f32[384]{0:T(512)S(1)}, f32[384]{0:T(512)}, u32[]{:S(2)}) copy-start(f32[384]{0:T(512)} %get-tuple-element.42) | copy-start | bytes 4612
  144.5 73.6 %copy-start.38 = (f32[1536]{0:T(1024)S(1)}, f32[1536]{0:T(1024)}, u32[]{:S(2)}) copy-start(f32[1536]{0:T(1024)} %get-tuple-element.70) | copy-start | bytes 18436
  144.5 73.7 %copy-start.56 = (f32[384]{0:T(512)S(1)}, f32[384]{0:T(512)}, u32[]{:S(2)}) copy-start(f32[384]{0:T(512)} %get-tuple-element.20) | copy-start | bytes 4612
  144.5 107.4 %copy-start.29 = (bf16[1344]{0:T(1024)(128)(2,1)S(1)}, bf16[1344]{0:T(1024)(128)(2,1)}, u32[]{:S(2)}) copy-start(bf16[1344]{0:T(1024)(128)(2,1)} %param.17) | copy-start | bytes 8068
  144.5 107.4 %copy-start.46 = (bf16[1344]{0:T(1024)(128)(2,1)S(1)}, bf16[1344]{0:T(1024)(128)(2,1)}, u32[]{:S(2)}) copy-start(bf16[1344]{0:T(1024)(128)(2,1)} %param.22) | copy-start | bytes 8068
  144.5 107.4 %copy-start.47 = (bf16[1344]{0:T(1024)(128)(2,1)S(1)}, bf16[1344]{0:T(1024)(128)(2,1)}, u32[]{:S(2)}) copy-start(bf16[1344]{0:T(1024)(128)(2,1)} %param.23) | copy-start | bytes 8068
  144.5 108.0 %copy-start.45 = (bf16[2,384]{1,0:T(2,128)(2,1)S(1)}, bf16[2,384]{1,0:T(2,128)(2,1)}, u32[]{:S(2)}) copy-start(bf16[2,384]{1,0:T(2,128)(2,1)} %param.13) | copy-start | bytes 4612
  144.6 193.9 %copy-start.16 = (bf16[384,384]{1,0:T(8,128)(2,1)S(1)}, bf16[384,384]{1,0:T(8,128)(2,1)}, u32[]{:S(2)}) copy-start(bf16[384,384]{1,0:T(8,128)(2,1)} %param.16) | copy-start | bytes 884740
  144.6 193.9 %all-reduce.5.cloned.1.call-start = ((), (), s32[]{:S(2)}) async-start(), calls=%async_computation.8 | async-start | bytes 5308416 | tf_op jit(solution)/shard_map/psum | solution.py:232
  217.2 124.2 %copy-start.1 = (bf16[96,5376]{1,0:T(8,128)(2,1)S(1)}, bf16[96,5376]{1,0:T(8,128)(2,1)}, u32[]{:S(2)}) copy-start(bf16[96,5376]{1,0:T(8,128)(2,1)} %param.15) | copy-start | bytes 3096580
  (53 other events, 148.2 us)
Sparse Core Ops, SparseCore 0:
  10.2 23.5 all-gather.4
  35.9 17.4 all-gather.6
  55.0 17.4 all-gather.8
  73.9 34.1 all-gather.10
  110.4 33.0 reduce-scatter.4
  146.2 70.8 reduce-scatter.2
  221.3 117.1 all-reduce.4
where the time goes:
time: 354 us; the launch traced here: 353 us
  waiting for transfers between devices  188 us (53%)
  blocking collectives  62.4 us (18%)
  matrix products  46 us (13%)
  local copies, waits for them, and re-layouts  23.2 us (7%)
  other arithmetic  16.7 us (5%)
  between operations  16.4 us (5%)
    psum x1, waiting for transfers between devices, per_device(): lax.psum((rows_share, down_share, bias_share), 'replica')  83.2 us
    reduce_scatter x1, waiting for transfers between devices, per_device(): lax.psum_scatter(total_rows, 'shard', scatter_dimension=0, tiled=True)  72.5 us
    dot_general x21, matrix products, matrix_multiply(): jnp.einsum(spec_text, left, right, preferred_element_type=jnp.float32)  46 us
    unnamed x2, blocking collectives  23.4 us
    psum x1, blocking collectives, per_device(): lax.psum((rows_share, down_share, bias_share), 'replica')  23.4 us
    all_gather x1, waiting for transfers between devices, per_device(): lax.all_gather(w_rows, 'shard', axis=0, tiled=True)  23.1 us
    all_gather x1, blocking collectives, per_device(): lax.all_gather(w_rows[:, six_width:9 * embedding_width], 'shard', axis=0,...  9.25 us
    sub x3, other arithmetic, adam_step(): master - learn_rate * (first_hat / (jnp.sqrt(second_hat) + adam_eps) + we...  8.76 us
  transfers between devices with their start and end apart: 7, of which 4 were waited for; matrix products, arithmetic and copies ran while one was open for 19% of the time, Pallas kernels for 0%

commit v1 on v0

--- a/solution.py
+++ b/solution.py
@@ -3,6 +3,8 @@
 import jax
 import jax.numpy as jnp
 from jax import lax
+from jax.experimental import pallas as pl
+from jax.experimental.pallas import tpu as pltpu
 from jax.sharding import PartitionSpec as P
 
 HEADS = 6
@@ -50,7 +52,456 @@
     return (updated, first_new, second_new)
 
 
+MESH = pl.DeviceIdType.MESH
+VMEM_BYTES = 56 * 1024 * 1024
+ROW_STEP = 144
+
+
+class Copies:
+    def __init__(self, send_sem, recv_sem):
+        self.send_sem, self.recv_sem, self.made = send_sem, recv_sem, []
+
+    def start(self, source, target, device):
+        at = len(self.made)
+        copy = pltpu.make_async_remote_copy(
+            src_ref=source,
+            dst_ref=target,
+            send_sem=self.send_sem.at[at],
+            recv_sem=self.recv_sem.at[at],
+            device_id=device,
+            device_id_type=MESH,
+        )
+        copy.start()
+        self.made.append(copy)
+        return copy
+
+    def finish(self):
+        for copy in self.made:
+            copy.wait_send()
+
+
+def meet(peers):
+    barrier = pltpu.get_barrier_semaphore()
+    for peer in peers:
+        pl.semaphore_signal(barrier, inc=1, device_id=peer, device_id_type=MESH)
+    pl.semaphore_wait(barrier, len(peers))
+
+
+def flip(index):
+    return index + 1 - 2 * lax.rem(index, 2)
+
+
+def gather_kernel(
+    rows_ref,
+    down_ref,
+    bias_ref,
+    cond_ref,
+    silu_ref,
+    rows_out,
+    down_out,
+    bias_out,
+    mod_out,
+    silu_all,
+    part,
+    part_in,
+    send_sem,
+    recv_sem,
+    own_sem,
+):
+    s, r = lax.axis_index("shard"), lax.axis_index("replica")
+    x = lax.rem(r, 2)
+    core, across, corner = (flip(s), r), (lax.rem(s + 2, 4), r), (flip(lax.rem(s + 2, 4)), r)
+    beside = (s, flip(r))
+    meet([core, across, corner, beside])
+    copies = Copies(send_sem, recv_sem)
+    far = across[0]
+    columns = rows_ref.shape[1]
+    half_rows, half_down = rows_ref.shape[0] // 2, down_ref.shape[0] // 2
+
+    silu_copies = [
+        copies.start(silu_ref.at[peer[0]], silu_all.at[s], peer) for peer in (across, corner, core)
+    ]
+
+    def pieces(slot, half):
+        low = pl.ds(pl.multiple_of(half * half_rows, 16), half_rows)
+        low_down = pl.ds(pl.multiple_of(half * half_down, 16), half_down)
+        found = []
+        for at in range(2):
+            cols = pl.ds(at * (columns // 2), columns // 2)
+            found.append((rows_ref.at[low, cols], rows_out.at[slot, low, cols]))
+        found.append((down_ref.at[low_down], down_out.at[slot, low_down]))
+        return found
+
+    bias_far = copies.start(bias_ref, bias_out.at[s], across)
+    first = [copies.start(source, target, across) for source, target in pieces(s, x)]
+    near = [
+        copies.start(bias_ref, bias_out.at[s], core),
+        copies.start(rows_ref, rows_out.at[s], core),
+        copies.start(down_ref, down_out.at[s], core),
+    ]
+    own = [
+        pltpu.make_async_copy(bias_ref, bias_out.at[s], own_sem.at[0]),
+        pltpu.make_async_copy(rows_ref, rows_out.at[s], own_sem.at[1]),
+        pltpu.make_async_copy(down_ref, down_out.at[s], own_sem.at[2]),
+    ]
+    for copy in own:
+        copy.start()
+
+    silu_all[s] = silu_ref[s]
+    for copy in silu_copies:
+        copy.wait_recv()
+    depth = cond_ref.shape[0]
+    width = part.shape[-1]
+    rows = silu_all.shape[0] * silu_all.shape[1]
+    left = silu_all[...].reshape(rows, silu_all.shape[2])[:, :depth]
+    row = lax.rem(lax.rem(lax.broadcasted_iota(jnp.int32, left.shape, 0), 16), 6)
+    total = jnp.zeros((rows, width), jnp.float32)
+    for block in range(6):
+        chosen = jnp.where(row == block, left, jnp.zeros_like(left))
+        total = total + jnp.dot(
+            chosen,
+            cond_ref[:, block * width : (block + 1) * width],
+            preferred_element_type=jnp.float32,
+        )
+    part[...] = total.reshape(part.shape)
+    mod_copies = [
+        copies.start(part.at[peer[0]], part_in.at[at], peer)
+        for at, peer in enumerate((across, corner, core))
+    ]
+
+    bias_far.wait_recv()
+    late = [copies.start(bias_out.at[far], bias_out.at[far], core)]
+    second = []
+    for copy, (_, target) in zip(first, pieces(far, x)):
+        copy.wait_recv()
+        second.append(copies.start(target, target, beside))
+        late.append(copies.start(target, target, core))
+    for copy, (_, target) in zip(second, pieces(far, 1 - x)):
+        copy.wait_recv()
+        late.append(copies.start(target, target, core))
+    for copy in mod_copies:
+        copy.wait_recv()
+    mod_out[...] = part[s] + part_in[0] + part_in[1] + part_in[2]
+    for copy in near + late:
+        copy.wait_recv()
+    for copy in own:
+        copy.wait()
+    copies.finish()
+
+
+def gather_weights(w_rows, w_down, bias_pack, silu_cond, shards, replicas):
+    latents, width = silu_cond.shape
+    own_rows, six_width = w_rows.shape[0], 6 * width
+    if shards != 4 or replicas != 8 or latents != 2:
+        cond_matrix = lax.all_gather(w_rows[:, :six_width], "shard", axis=0, tiled=True)
+        return (
+            lax.all_gather(w_rows[:, six_width:], "shard", axis=0, tiled=True),
+            lax.all_gather(w_down, "shard", axis=0, tiled=True),
+            lax.all_gather(bias_pack, "shard", axis=0, tiled=True),
+            matrix_multiply("ld,de->le", silu_cond, cond_matrix),
+        )
+    spread = silu_cond.reshape(latents, shards, own_rows).transpose(1, 0, 2)
+    spread = jnp.repeat(spread, 6, axis=1)
+    spread = jnp.pad(spread, ((0, 0), (0, 16 - 6 * latents), (0, 128 - own_rows)))
+    bias_tile = jnp.pad(bias_pack, (0, 2048 - bias_pack.shape[0])).reshape(16, 128)
+    rows = w_rows[:, six_width:]
+    vmem = pl.BlockSpec(memory_space=pltpu.VMEM)
+    rows_full, down_full, bias_full, mod = pl.pallas_call(
+        gather_kernel,
+        out_shape=(
+            jax.ShapeDtypeStruct((shards,) + rows.shape, jnp.bfloat16),
+            jax.ShapeDtypeStruct((shards,) + w_down.shape, jnp.bfloat16),
+            jax.ShapeDtypeStruct((shards, 16, 128), jnp.bfloat16),
+            jax.ShapeDtypeStruct((16, width), jnp.float32),
+        ),
+        in_specs=[vmem] * 5,
+        out_specs=(vmem,) * 4,
+        scratch_shapes=[
+            pltpu.VMEM((shards, 16, 128), jnp.bfloat16),
+            pltpu.VMEM((shards, 16, width), jnp.float32),
+            pltpu.VMEM((3, 16, width), jnp.float32),
+            pltpu.SemaphoreType.DMA((32,)),
+            pltpu.SemaphoreType.DMA((32,)),
+            pltpu.SemaphoreType.DMA((3,)),
+        ],
+        compiler_params=pltpu.CompilerParams(
+            collective_id=0, has_side_effects=True, vmem_limit_bytes=VMEM_BYTES
+        ),
+        name="gather_weights",
+    )(rows, w_down, bias_tile, w_rows[:, :six_width], spread)
+    bias_full = bias_full.reshape(shards, 2048)[:, : bias_pack.shape[0]].reshape(-1)
+    return (
+        rows_full.reshape(-1, rows.shape[1]),
+        down_full.reshape(-1, width),
+        bias_full,
+        mod[: 6 * latents].reshape(latents, six_width),
+    )
+
+
+def reduce_kernel(
+    packed_ref,
+    small_ref,
+    cond_ref,
+    sum_out,
+    small_out,
+    silu_out,
+    core_in,
+    core_sum,
+    across_in,
+    across_sum,
+    beside_in,
+    beside_sum,
+    line_in,
+    silu_part,
+    send_sem,
+    recv_sem,
+):
+    s, r = lax.axis_index("shard"), lax.axis_index("replica")
+    x, z = lax.rem(r, 2), r // 2
+    c, y = lax.rem(s, 2), s // 2
+    core, across, corner = (flip(s), r), (lax.rem(s + 2, 4), r), (flip(lax.rem(s + 2, 4)), r)
+    beside = (s, flip(r))
+    line_z = [lax.rem(z + step, 4) for step in (1, 2, 3)]
+    line = [(s, 2 * at + x) for at in line_z]
+    meet([core, across, corner, beside] + line)
+    copies = Copies(send_sem, recv_sem)
+    parts = range(3)
+    cols = [pl.ds(128 * part, 128) for part in parts]
+    whole = packed_ref.shape[1]
+    half, share = whole // 2, whole // 8
+
+    def add_rows(count, body):
+        def one(step, carry):
+            body(pl.multiple_of(step * ROW_STEP, 16))
+            return carry
+
+        lax.fori_loop(0, count // ROW_STEP, one, 0)
+
+    def f32(value):
+        return value.astype(jnp.float32)
+
+    core_copies = []
+    for part in parts:
+        core_copies.append(
+            [
+                copies.start(
+                    packed_ref.at[2 * side + 1 - c, :, cols[part]],
+                    core_in.at[side, :, cols[part]],
+                    core,
+                )
+                for side in (1 - y, y)
+            ]
+        )
+    small_out[s, x, z] = small_ref[...]
+    own_small = small_out.at[s, x, z]
+    small_line = [copies.start(own_small, own_small, peer) for peer in line]
+
+    across_copies = []
+    for part in parts:
+        for at, side in enumerate((1 - y, y)):
+            core_copies[part][at].wait_recv()
+
+            def add(low, part=part, side=side):
+                rows = pl.ds(low, ROW_STEP)
+                core_sum[side, rows, cols[part]] = (
+                    f32(packed_ref[2 * side + c, rows, cols[part]])
+                    + f32(core_in[side, rows, cols[part]])
+                ).astype(jnp.bfloat16)
+
+            add_rows(whole, add)
+            if at == 0:
+                across_copies.append(
+                    copies.start(
+                        core_sum.at[side, :, cols[part]], across_in.at[:, cols[part]], across
+                    )
+                )
+
+    for copy in small_line:
+        copy.wait_recv()
+    small_beside = copies.start(small_out.at[s, x], small_out.at[s, x], beside)
+
+    beside_copies, line_copies, gather_copies, last_copies = {}, {}, {}, {}
+
+    def stage_beside(part):
+        across_copies[part].wait_recv()
+
+        def add(low):
+            rows = pl.ds(low, ROW_STEP)
+            across_sum[rows, cols[part]] = (
+                f32(core_sum[y, rows, cols[part]]) + f32(across_in[rows, cols[part]])
+            ).astype(jnp.bfloat16)
+
+        add_rows(whole, add)
+        beside_copies[part] = copies.start(
+            across_sum.at[pl.ds(pl.multiple_of((1 - x) * half, 16), half), cols[part]],
+            beside_in.at[:, cols[part]],
+            beside,
+        )
+
+    def stage_line(part):
+        beside_copies[part].wait_recv()
+
+        def add(low):
+            rows = pl.ds(low, ROW_STEP)
+            from_rows = pl.ds(pl.multiple_of(x * half + low, 16), ROW_STEP)
+            beside_sum[rows, cols[part]] = (
+                f32(across_sum[from_rows, cols[part]]) + f32(beside_in[rows, cols[part]])
+            ).astype(jnp.bfloat16)
+
+        add_rows(half, add)
+        line_copies[part] = [
+            copies.start(
+                beside_sum.at[pl.ds(pl.multiple_of(line_z[at] * share, 16), share), cols[part]],
+                line_in.at[at, :, cols[part]],
+                line[at],
+            )
+            for at in range(3)
+        ]
+
+    def stage_gather(part):
+        for copy in line_copies[part]:
+            copy.wait_recv()
+        rows = pl.ds(pl.multiple_of(z * share, 16), share)
+        total = f32(beside_sum[rows, cols[part]])
+        for at in range(3):
+            total = total + f32(line_in[at, :, cols[part]])
+        sum_out[x, z, :, cols[part]] = total.astype(jnp.bfloat16)
+        own = sum_out.at[x, z, :, cols[part]]
+        gather_copies[part] = [copies.start(own, own, peer) for peer in line]
+        last_copies[part] = [copies.start(own, own, beside)]
+
+    def stage_last(part):
+        for at in range(3):
+            gather_copies[part][at].wait_recv()
+            origin = lax.rem(z + 3 - at, 4)
+            piece = sum_out.at[x, origin, :, cols[part]]
+            last_copies[part].append(copies.start(piece, piece, beside))
+
+    stage_beside(0)
+    small_beside.wait_recv()
+    small_across = copies.start(small_out.at[s], small_out.at[s], across)
+    stage_beside(1)
+    stage_line(0)
+    stage_beside(2)
+    stage_line(1)
+    stage_gather(0)
+    small_across.wait_recv()
+    far = across[0]
+    small_core = [
+        copies.start(small_out.at[s], small_out.at[s], core),
+        copies.start(small_out.at[far], small_out.at[far], core),
+    ]
+    stage_line(2)
+    stage_gather(1)
+    stage_last(0)
+
+    for copy in small_core:
+        copy.wait_recv()
+    depth = cond_ref.shape[0]
+    width = packed_ref.shape[-1]
+    left = jnp.concatenate([small_out[at, x, z, 0:16] for at in range(4)], axis=0)
+    row = lax.rem(lax.rem(lax.broadcasted_iota(jnp.int32, left.shape, 0), 16), 6)
+    total = jnp.zeros((64, depth), jnp.float32)
+    for block in range(6):
+        chosen = jnp.where(row == block, left, jnp.zeros_like(left))
+        total = total + lax.dot_general(
+            chosen,
+            cond_ref[:, block * width : (block + 1) * width],
+            (((1,), (1,)), ((), ())),
+            preferred_element_type=jnp.float32,
+        )
+    silu_part[...] = jnp.zeros_like(silu_part)
+    silu_part[:, :, 0:depth] = total.reshape(4, 16, depth)
+    silu_out[s] = silu_part[s]
+    silu_copies = [
+        copies.start(silu_part.at[peer[0]], silu_out.at[s], peer)
+        for peer in (across, corner, core)
+    ]
+    stage_gather(2)
+    stage_last(1)
+    stage_last(2)
+    for copy in silu_copies:
+        copy.wait_recv()
+    for part in parts:
+        for copy in last_copies[part]:
+            copy.wait_recv()
+    copies.finish()
+
+
+def reduce_gradients(
+    packed, delta_modulation, silu_cond, bias_local, w_rows, shards, replicas
+):
+    latents, width = silu_cond.shape
+    own_rows, six_width = w_rows.shape[0], 6 * width
+    if shards != 4 or replicas != 8 or latents != 2:
+        summed = lax.psum_scatter(
+            packed.reshape(-1, width).astype(jnp.float32), "shard", scatter_dimension=0, tiled=True
+        )
+        summed = lax.psum(summed, "replica")
+        axes = ("shard", "replica")
+        cond_matrix = lax.all_gather(w_rows[:, :six_width], "shard", axis=0, tiled=True)
+        return (
+            summed,
+            lax.all_gather(delta_modulation, axes, axis=0, tiled=True),
+            lax.all_gather(silu_cond, axes, axis=0, tiled=True),
+            lax.psum(bias_local, axes),
+            matrix_multiply("le,de->ld", delta_modulation, cond_matrix),
+        )
+    whole = packed.shape[1]
+    small = jnp.concatenate(
+        [
+            delta_modulation.reshape(6 * latents, width),
+            silu_cond,
+            jnp.zeros((16 - 7 * latents, width), jnp.bfloat16),
+            bias_local.astype(jnp.bfloat16).reshape(-1, width),
+            jnp.zeros((16 - bias_local.shape[0] // width, width), jnp.bfloat16),
+        ],
+        axis=0,
+    )
+    vmem = pl.BlockSpec(memory_space=pltpu.VMEM)
+    bf16 = jnp.bfloat16
+    summed, every, silu_parts = pl.pallas_call(
+        reduce_kernel,
+        out_shape=(
+            jax.ShapeDtypeStruct((2, 4, whole // 8, width), bf16),
+            jax.ShapeDtypeStruct((shards, 2, 4, 32, width), bf16),
+            jax.ShapeDtypeStruct((shards, 16, 128), jnp.float32),
+        ),
+        in_specs=[vmem] * 3,
+        out_specs=(vmem,) * 3,
+        scratch_shapes=[
+            pltpu.VMEM((2, whole, width), bf16),
+            pltpu.VMEM((2, whole, width), bf16),
+            pltpu.VMEM((whole, width), bf16),
+            pltpu.VMEM((whole, width), bf16),
+            pltpu.VMEM((whole // 2, width), bf16),
+            pltpu.VMEM((whole // 2, width), bf16),
+            pltpu.VMEM((3, whole // 8, width), bf16),
+            pltpu.VMEM((shards, 16, 128), jnp.float32),
+            pltpu.SemaphoreType.DMA((64,)),
+            pltpu.SemaphoreType.DMA((64,)),
+        ],
+        compiler_params=pltpu.CompilerParams(
+            collective_id=1, has_side_effects=True, vmem_limit_bytes=VMEM_BYTES
+        ),
+        name="reduce_gradients",
+    )(packed, small, w_rows[:, :six_width])
+    every = every.transpose(0, 2, 1, 3, 4).reshape(shards * replicas, 32, width)
+    bias_rows = every[:, 16 : 16 + bias_local.shape[0] // width]
+    delta_silu = silu_parts[:, : 6 * latents, :own_rows]
+    delta_silu = delta_silu.reshape(shards, latents, 6, own_rows).sum(axis=2)
+    return (
+        summed.reshape(whole, width),
+        every[:, : 6 * latents].reshape(-1, six_width),
+        every[:, 6 * latents : 7 * latents].reshape(-1, width),
+        bias_rows.astype(jnp.float32).sum(axis=0).reshape(-1),
+        delta_silu.transpose(1, 0, 2).reshape(latents, width),
+    )
+
+
 def per_device(
+    shards,
+    replicas,
     tokens,
     condition,
     cotangent,
@@ -67,25 +518,21 @@
     latents, positions, embedding_width = tokens.shape
     hidden_units_width = w_rows.shape[1] - 10 * embedding_width
     six_width = 6 * embedding_width
-    cond_matrix, bias_full = (
-        lax.all_gather(w_rows[:, :six_width], "shard", axis=0, tiled=True),
-        lax.all_gather(bias_pack, "shard", axis=0, tiled=True),
-    )
-    bias_entries = bias_full.astype(jnp.float32)
     cond_values = condition.astype(jnp.float32)
     silu_cond = jax.nn.silu(cond_values).astype(jnp.bfloat16)
-    modulation = matrix_multiply("ld,de->le", silu_cond, cond_matrix) + bias_entries[:six_width]
+    rows_full, shrink_weight, bias_full, modulation = gather_weights(
+        w_rows, w_down, bias_pack, silu_cond, shards, replicas
+    )
+    bias_entries = bias_full.astype(jnp.float32)
+    modulation = modulation + bias_entries[:six_width]
+    triple_matrix = rows_full[:, : 3 * embedding_width]
+    output_matrix = rows_full[:, 3 * embedding_width : 4 * embedding_width]
+    expand_weight = rows_full[:, 4 * embedding_width :]
     blocks_six = [
         modulation[:, None, index * embedding_width : (index + 1) * embedding_width]
         for index in range(6)
     ]
     shift_attention, scale_attention, gate_attention, shift_feed, scale_feed, gate_feed = blocks_six
-    triple_matrix, output_matrix = (
-        lax.all_gather(w_rows[:, six_width : 9 * embedding_width], "shard", axis=0, tiled=True),
-        lax.all_gather(
-            w_rows[:, 9 * embedding_width : 10 * embedding_width], "shard", axis=0, tiled=True
-        ),
-    )
     token_values = tokens.astype(jnp.float32)
     normed_attention, inv_attention = normalize(token_values)
     input_attention = (normed_attention * (1.0 + scale_attention) + shift_attention).astype(
@@ -123,10 +570,6 @@
     residual = token_values + gate_attention * branch
     normed_feed, inv_feed = normalize(residual)
     feed_input = (normed_feed * (1.0 + scale_feed) + shift_feed).astype(jnp.bfloat16)
-    expand_weight, shrink_weight = (
-        lax.all_gather(w_rows[:, 10 * embedding_width :], "shard", axis=0, tiled=True),
-        lax.all_gather(w_down, "shard", axis=0, tiled=True),
-    )
     hidden = (
         matrix_multiply("wqg,gc->wqc", feed_input, expand_weight)
         + bias_entries[9 * embedding_width : 9 * embedding_width + hidden_units_width]
@@ -138,14 +581,6 @@
         + bias_entries[9 * embedding_width + hidden_units_width :]
     )
     block_out = (residual + gate_feed * feed_out).astype(jnp.bfloat16)
-    rows_whole, shrink_weight = (
-        lax.all_gather(w_rows, "shard", axis=0, tiled=True),
-        lax.all_gather(w_down, "shard", axis=0, tiled=True),
-    )
-    cond_matrix = rows_whole[:, :six_width]
-    triple_matrix = rows_whole[:, six_width : 9 * embedding_width]
-    output_matrix = rows_whole[:, 9 * embedding_width : 10 * embedding_width]
-    expand_weight = rows_whole[:, 10 * embedding_width :]
     upstream = cotangent.astype(jnp.float32)
     delta_gate_feed = jnp.sum(upstream * feed_out, axis=1)
     delta_feed_branch = (gate_feed * upstream).astype(jnp.bfloat16)
@@ -214,22 +649,40 @@
         ],
         axis=1,
     ).astype(jnp.bfloat16)
-    total_cond = matrix_multiply("ld,le->de", silu_cond, delta_modulation)
-    bias_cond = jnp.sum(delta_modulation.astype(jnp.float32), axis=0)
-    delta_silu = matrix_multiply("le,de->ld", delta_modulation, cond_matrix)
+    bias_local = jnp.concatenate([bias_query, bias_valued, bias_output, bias_expand, bias_down])
+    total_rows = jnp.concatenate([total_triple, total_output, summed_expand_weight], axis=1)
+    blocks = total_rows.shape[1] // embedding_width
+    shard_rows = w_rows.shape[0]
+    packed_rows = (
+        total_rows.astype(jnp.bfloat16)
+        .reshape(shards, shard_rows, blocks, embedding_width)
+        .transpose(0, 2, 1, 3)
+        .reshape(shards, blocks * shard_rows, embedding_width)
+    )
+    packed_down = summed_down_weight.astype(jnp.bfloat16).reshape(shards, -1, embedding_width)
+    packed = jnp.concatenate([packed_rows, packed_down], axis=1)
+    summed, every_modulation, every_silu, bias_rest, delta_silu = reduce_gradients(
+        packed, delta_modulation, silu_cond, bias_local, w_rows, shards, replicas
+    )
+    shard_at = lax.axis_index("shard")
+    own_silu = lax.dynamic_slice_in_dim(every_silu, shard_at * shard_rows, shard_rows, 1)
+    total_cond = matrix_multiply("ld,le->de", own_silu, every_modulation)
+    bias_cond = jnp.sum(every_modulation.astype(jnp.float32), axis=0)
     cond_grad = jax.vjp(jax.nn.silu, cond_values)[1](delta_silu)[0]
-    total_bias = jnp.concatenate(
-        [bias_cond, bias_query, bias_valued, bias_output, bias_expand, bias_down]
-    )
-    total_rows = jnp.concatenate(
-        [total_cond, total_triple, total_output, summed_expand_weight], axis=1
-    )
-    rows_share, down_share, bias_share = (
-        lax.psum_scatter(total_rows, "shard", scatter_dimension=0, tiled=True),
-        lax.psum_scatter(summed_down_weight, "shard", scatter_dimension=0, tiled=True),
-        lax.psum_scatter(total_bias, "shard", scatter_dimension=0, tiled=True),
-    )
-    rows_grad, down_grad, bias_grad = lax.psum((rows_share, down_share, bias_share), "replica")
+    split_at = blocks * shard_rows
+    own_rows = (
+        summed[:split_at]
+        .reshape(blocks, shard_rows, embedding_width)
+        .transpose(1, 0, 2)
+        .reshape(shard_rows, -1)
+        .astype(jnp.float32)
+    )
+    rows_grad = jnp.concatenate([total_cond, own_rows], axis=1)
+    down_grad = summed[split_at:].astype(jnp.float32)
+    bias_share = bias_pack.shape[0]
+    bias_grad = lax.dynamic_slice_in_dim(
+        jnp.concatenate([bias_cond, bias_rest]), shard_at * bias_share, bias_share, 0
+    )
     rows_new, rows_first_new, rows_second_new = adam_step(
         w_rows, rows_grad, rows_first, rows_second, decay_rate
     )
@@ -271,7 +724,7 @@
         P("shard"),
     )
     return jax.shard_map(
-        per_device,
+        partial(per_device, mesh.shape["shard"], mesh.shape["replica"]),
         mesh=mesh,
         in_specs=placed,
         out_specs=(

time: 354 us -> 161 us (0.45)
  waiting for transfers between devices: 188 us -> 0 us
  Pallas kernels: 0 us -> 77 us
  blocking collectives: 62.4 us -> 0 us
  between operations: 16.4 us -> 1.44 us
  matrix products: 46 us -> 31.6 us
  local copies, waits for them, and re-layouts: 23.2 us -> 32.1 us
    psum x1 -> x0, waiting for transfers between devices: 83.2 us -> none  [per_device(): lax.psum((rows_share, down_share, bias_share), 'replica')]
    pallas_call x0 -> x2, Pallas kernels: none -> 77 us  [the longest x1 52.9 us: reduce_gradients(): pl.pallas_call(reduce_kernel, out_shape=(jax.ShapeDtypeStruct((2, 4, whol...]
    reduce_scatter x2 -> x0, waiting for transfers between devices: 72.5 us -> none  [the longest x1 72.5 us: per_device(): lax.psum_scatter(total_rows, 'shard', scatter_dimension=0, tiled=True)]
    all_gather x4 -> x0, waiting for transfers between devices: 31.3 us -> none  [the longest x1 23.1 us: per_device(): lax.all_gather(w_rows, 'shard', axis=0, tiled=True)]
    unnamed x2 -> x0, blocking collectives: 23.4 us -> none
    psum x1 -> x0, blocking collectives: 23.4 us -> none  [per_device(): lax.psum((rows_share, down_share, bias_share), 'replica')]
    all_gather x2 -> x0, blocking collectives: 15.6 us -> none  [the longest x1 9.25 us: per_device(): lax.all_gather(w_rows[:, six_width:9 * embedding_width], 'shard', axis=0,...]
    dot_general x21 -> x19, matrix products: 46 us -> 31.6 us  [matrix_multiply(): jnp.einsum(spec_text, left, right, preferred_element_type=jnp.float32)]
  transfers between devices with their start and end apart: 7 -> 0, of which waited for: 4 -> 0; matrix products, arithmetic and copies ran while one was open for 19% -> 0% of each run, Pallas kernels for 0% -> 0%
where the time goes in v1:
time: 161 us; the launch traced here: 160 us
  Pallas kernels  77 us (48%)
  local copies, waits for them, and re-layouts  32.1 us (20%)
  matrix products  31.6 us (20%)
  other arithmetic  17.7 us (11%)
    pallas_call x1, Pallas kernels, reduce_gradients(): pl.pallas_call(reduce_kernel, out_shape=(jax.ShapeDtypeStruct((2, 4, whol...  52.9 us
    dot_general x19, matrix products, matrix_multiply(): jnp.einsum(spec_text, left, right, preferred_element_type=jnp.float32)  31.6 us
    pallas_call x1, Pallas kernels, gather_weights(): pl.pallas_call(gather_kernel, out_shape=(jax.ShapeDtypeStruct((shards,) +...  24 us
    unnamed x111, local copies, waits for them, and re-layouts  7.49 us
    sub x3, other arithmetic, adam_step(): master - learn_rate * (first_hat / (jnp.sqrt(second_hat) + adam_eps) + we...  6.01 us

profile of v1, /device:TPU:0, one launch (start us, length us, event | category | flops | bytes accessed | tf_op | source)
XLA Modules:
  0.0 159.9 jit_solution(9555503476858750320)
XLA Ops:
  5.9 1.8 %slice.86.cond_ref = bf16[96,2304]{1,0:T(8,128)(2,1)} slice(bf16[96,5376]{1,0:T(8,128)(2,1)} %param.15), slice={[0:96], [0:2304]} | slice | bytes 884736 | tf_op jit(solution)/shard_map/slice | solution.py:231
  7.7 1.9 %slice.85.rows_ref = bf16[96,3072]{1,0:T(8,128)(2,1)} slice(bf16[96,5376]{1,0:T(8,128)(2,1)} %param.15), slice={[0:96], [2304:5376]} | slice | bytes 1179648 | tf_op jit(solution)/shard_map/slice | solution.py:207
  9.6 24.0 %gather_weights.1 = (bf16[4,96,3072]{2,1,0:T(8,128)(2,1)}, bf16[4,384,384]{2,1,0:T(8,128)(2,1)}, bf16[4,16,128]{2,1,0:T(8,128)(2,1)}, f32[16,384]{1,0:T(8,128)}) custom-call(bf16[96,3072]{1,0:T(8,128)(2,1)} %slice.85.rows_ref, bf16[384,384]{1,0:T(8,128)(2,1)} %down_ref.1, bf16[16,128]{1,0:T(8,128)(2,1)} %pad_bitcast_fusion.bias_ref, ...), custom_call_target="tpu_custom_call" | custom-call | tf_op jit(solution)/shard_map/gather_weights/pallas_call | solution.py:209
  37.6 2.1 %fusion.7 = bf16[2,256,1152]{2,1,0:T(8,128)(2,1)S(1)} fusion(f32[1152]{0:T(1024)S(1)} %pad_maximum_fusion.6, bf16[384,3072]{1,0:T(8,128)(2,1)} %bitcast.126, bf16[2,256,384]{2,1,0:T(8,128)(2,1)S(1)} %copy-done, f32[2,384]{1,0:T(2,128)S(1)} %get-tuple-element.67, f32[2,384]{1,0:T(2,128)S(1)} %get-tuple-element.68, f32[2,256]{1,0:T(2,128)S(1)} %add_rsqrt_fusion.1, ...), kind=kOutput, calls=%fused_computation.18 | convolution fusion | flops 455344128 | bytes 2472448 | tf_op jit(solution)/shard_map/lsd,de->lse/dot_general | solution.py:40
  42.6 1.7 %multiply_reduce_fusion.1 = (f32[2,6,256]{2,1,0:T(8,128)S(1)}, f32[2,6,256,256]{2,3,1,0:T(8,128)S(1)}) fusion(bf16[2,256,6,64]{1,3,2,0:T(8,128)(2,1)} %bitcast.107, bf16[2,256,6,64]{1,3,2,0:T(8,128)(2,1)} %bitcast.111), kind=kOutput, calls=%fused_computation.25 | convolution fusion | flops 102233088 | bytes 3944448 | tf_op jit(solution)/shard_map/lqhe,lkhe->lhqk/dot_general | solution.py:40
  46.6 1.4 fusion.70
  49.4 2.5 %fusion.9 = bf16[1536,384]{1,0:T(8,128)(2,1)} fusion(bf16[2,256,384]{2,1,0:T(8,128)(2,1)S(1)} %copy-done.15, f32[2,384]{1,0:T(2,128)S(1)} %copy-done.26, f32[2,256,1536]{2,1,0:T(8,128)S(1)} %convolution_add_fusion.1), kind=kOutput, calls=%fused_computation.23 | convolution fusion | flops 612237312 | bytes 4721664 | tf_op jit(solution)/shard_map/pxz,pxk->zk/dot_general | solution.py:40
  51.9 3.4 %fusion.74 = (bf16[1536]{0:T(1024)(128)(2,1)}, bf16[2,256,1536]{2,1,0:T(8,128)(2,1)S(1)}) fusion(f32[2,256,1536]{2,1,0:T(8,128)S(1)} %convolution_add_fusion.1, bf16[1536,384,1]{1,0,2:T(8,128)(2,1)S(1)} %bitcast.140, bf16[2,256,384]{2,1,0:T(8,128)(2,1)S(1)} %copy-done.15, f32[2,384]{1,0:T(2,128)S(1)} %copy-done.26), kind=kOutput, calls=%fused_computation.154 | convolution fusion | flops 621083136 | bytes 6297600 | tf_op jit(solution)/shard_map/tgw,uw->tgu/dot_general | solution.py:40
  56.3 2.9 %fusion.35 = (bf16[2,384]{1,0:T(2,128)(2,1)}, bf16[2,256,384]{2,1,0:T(8,128)(2,1)}, bf16[2,384]{1,0:T(2,128)(2,1)}, f32[2,256]{1,0:T(2,128)S(1)}, f32[2,256]{1,0:T(2,128)S(1)}, /*index=5*/bf16[2,384]{1,0:T(2,128)(2,1)}) fusion(bf16[2,256,384]{2,1,0:T(8,128)(2,1)S(1)} %copy-done.15, f32[2,256,384]{2,1,0:T(8,128)S(1)} %get-tuple-element.47, ...), kind=kOutput, calls=%fused_computation.74 | convolution fusion | flops 614200064 | bytes 6705152 | tf_op jit(solution)/shard_map/wku,ux->wkx/dot_general | solution.py:40
  59.2 1.9 %fusion.8 = bf16[384,1536]{1,0:T(8,128)(2,1)} fusion(bf16[2,256,1536]{2,1,0:T(8,128)(2,1)S(1)} %get-tuple-element.81, f32[2,256,384]{2,1,0:T(8,128)S(1)} %get-tuple-element.47, f32[2,384]{1,0:T(2,128)S(1)} %copy-done.44, f32[2,384]{1,0:T(2,128)S(1)} %copy-done.27, f32[2,256]{1,0:T(2,128)S(1)} %add_rsqrt_fusion, f32[2,256]{1,0:T(2,128)S(1)} %broadcast_multiply_fusion.4), kind=kOutput, calls=%fused_computation.22 | convolution fusion | flops 605552640 | bytes 3549184 | tf_op jit(solution)/shard_map/pce,pcw->ew/dot_general | solution.py:40
  61.2 1.9 %fusion.69 = (bf16[384]{0:T(512)(128)(2,1)}, bf16[2,256,384]{2,1,0:T(8,128)(2,1)S(1)}, f32[2,256,384]{2,1,0:T(8,128)}, bf16[384]{0:T(512)(128)(2,1)}) fusion(f32[2,384]{1,0:T(2,128)S(1)} %copy-done.20, f32[2,256]{1,0:T(2,128)S(1)} %get-tuple-element.82, f32[2,256,384]{2,1,0:T(8,128)S(1)} %get-tuple-element.47, f32[2,256]{1,0:T(2,128)S(1)} %broadcast_multiply_fusion.4, ...), kind=kLoop, calls=%fused_computation.149 | loop fusion | flops 2948352 | bytes 3164672 | tf_op jit(solution)/shard_map/reduce_sum | solution.py:602
  65.0 1.8 %copy.66 = bf16[384,384]{1,0:T(8,128)(2,1)} copy(bf16[384,384]{0,1:T(8,128)(2,1)} %fusion.17) | data formatting | bytes 589824 | tf_op jit(solution)/shard_map/convert.18
  66.9 2.2 %convolution_convert_fusion.2 = bf16[2,256,384]{2,1,0:T(8,128)(2,1)} fusion(bf16[2,256,384]{2,1,0:T(8,128)(2,1)} %copy-done.2, bf16[384,3072]{1,0:T(8,128)(2,1)} %bitcast.127), kind=kOutput, calls=%fused_computation.44 | convolution fusion | flops 151191552 | bytes 1081344 | tf_op jit(solution)/shard_map/lse,de->lsd/dot_general | solution.py:40
  69.1 1.9 %copy.55 = bf16[2,256,384]{1,2,0:T(8,128)(2,1)} copy(bf16[2,256,384]{2,1,0:T(8,128)(2,1)} %convolution_convert_fusion.2) | data formatting | bytes 786432 | tf_op jit(solution)/shard_map/convert_element_type | solution.py:605
  71.0 3.0 %bitcast_reduce_fusion = (bf16[6,64]{1,0:T(8,128)(2,1)}, bf16[2,6,64,256]{3,2,1,0:T(8,128)(2,1)}) fusion(bf16[2,256,6,64]{1,3,2,0:T(8,128)(2,1)} %bitcast.105, f32[2,6,256,256]{2,3,1,0:T(8,128)S(1)} %get-tuple-element.71, f32[2,6,256]{2,1,0:T(8,128)S(1)} %log_add_fusion), kind=kOutput, calls=%fused_computation.94 | convolution fusion | flops 103415424 | bytes 3945216 | tf_op jit(solution)/shard_map/lhqk,lqhe->lkhe/dot_general | solution.py:40
  75.3 1.9 %copy.61 = bf16[2,256,384]{2,1,0:T(8,128)(2,1)} copy(bf16[2,256,384]{1,2,0:T(8,128)(2,1)} %bitcast.120) | data formatting | bytes 786432 | tf_op jit(solution)/shard_map/reshape | solution.py:627
  77.2 2.0 %multiply_reduce_fusion = (f32[2,6,256]{2,1,0:T(8,128)S(1)}, f32[2,6,256,256]{2,3,1,0:T(8,128)S(1)}) fusion(f32[2,6,256,256]{2,3,1,0:T(8,128)S(1)} %get-tuple-element.71, f32[2,6,256]{2,1,0:T(8,128)S(1)} %log_add_fusion, bf16[2,256,6,64]{1,3,2,0:T(8,128)(2,1)} %bitcast.106, bf16[2,256,6,64]{1,3,2,0:T(8,128)(2,1)} %bitcast.109), kind=kOutput, calls=%fused_computation.13 | convolution fusion | flops 103805952 | bytes 7102464 | tf_op jit(solution)/shard_map/lqhe,lkhe->lhqk/dot_general | solution.py:40
  83.4 2.3 %fusion.32 = (bf16[2,384]{1,0:T(2,128)(2,1)S(1)}, f32[2,256]{1,0:T(2,128)S(1)}, f32[2,256]{1,0:T(2,128)S(1)}, bf16[2,384]{1,0:T(2,128)(2,1)S(1)}, f32[2,256,384]{2,1,0:T(8,128)S(1)}) fusion(bf16[2,256,384]{2,1,0:T(8,128)(2,1)S(1)} %copy-done, f32[2,256]{1,0:T(2,128)S(1)} %copy-done.32, f32[2,256]{1,0:T(2,128)S(1)} %copy-done.22, ...), kind=kOutput, calls=%fused_computation.71 | convolution fusion | flops 458487296 | bytes 3258368 | tf_op jit(solution)/shard_map/lse,de->lsd/dot_general | solution.py:40
  89.2 2.1 %pad_maximum_fusion.packed_ref = bf16[4,1152,384]{2,1,0:T(8,128)(2,1)} fusion(bf16[4,384,384]{2,1,0:T(8,128)(2,1)S(1)} %bitcast.122, bf16[4,768,384]{2,1,0:T(8,128)(2,1)S(1)} %bitcast.101), kind=kLoop, calls=%fused_computation.2 | loop fusion | flops 7077888 | bytes 7077888 | tf_op jit(solution)/shard_map/concatenate | solution.py:663
  92.7 3.1 %concatenate.36.small_ref = bf16[32,384]{1,0:T(8,128)(2,1)} concatenate(bf16[12,384]{1,0:T(8,128)(2,1)S(1)} %convert_element_type.198, bf16[2,384]{1,0:T(2,128)(2,1)S(1)} %copy-done.25, bf16[2,384]{1,0:T(2,128)(2,1)S(1)} %broadcast_in_dim.13, bf16[8,384]{1,0:T(8,128)(2,1)S(1)} %convert_element_type.204, bf16[8,384]{1,0:T(8,128)(2,1)S(1)} %broadcast_in_dim.14), dimensions={0} | concatenate | bytes 49152 | tf_op jit(solution)/shard_map/concatenate | solution.py:451
  95.8 52.9 %reduce_gradients.1 = (bf16[2,4,144,384]{3,2,1,0:T(8,128)(2,1)}, bf16[4,2,4,32,384]{4,3,2,1,0:T(8,128)(2,1)}, f32[4,16,128]{2,1,0:T(8,128)}) custom-call(bf16[4,1152,384]{2,1,0:T(8,128)(2,1)} %pad_maximum_fusion.packed_ref, bf16[32,384]{1,0:T(8,128)(2,1)} %concatenate.36.small_ref, bf16[96,2304]{1,0:T(8,128)(2,1)} %slice.86.cond_ref), custom_call_target="tpu_custom_call" | custom-call | tf_op jit(solution)/shard_map/reduce_gradients/pallas_call | solution.py:463
  150.3 1.3 copy.70
  154.5 1.5 convert_subtract_fusion.2
  156.1 3.8 %convert_subtract_fusion = (f32[96,5376]{1,0:T(8,128)}, f32[96,5376]{1,0:T(8,128)}, f32[96,5376]{1,0:T(8,128)}) fusion(bf16[96,5376]{1,0:T(8,128)(2,1)S(1)} %copy-done.1, f32[96,3072]{1,0:T(8,128)S(1)} %bitcast.104, f32[96,2304]{1,0:T(8,128)S(1)} %fusion.48, bf16[96,5376]{1,0:T(8,128)(2,1)S(1)} %copy-done.12, bf16[96,5376]{1,0:T(8,128)(2,1)S(1)} %copy-done.13), kind=kLoop, calls=%fused_computation.26 | loop fusion | flops 9805824 | bytes 11354112 | tf_op jit(solution)/shard_map/sub | solution.py:49
  (182 shorter events, 32.8 us)
Async XLA Ops:
  0.6 37.0 %copy-start = (bf16[2,256,384]{2,1,0:T(8,128)(2,1)S(1)}, bf16[2,256,384]{2,1,0:T(8,128)(2,1)}, u32[]{:S(2)}) copy-start(bf16[2,256,384]{2,1,0:T(8,128)(2,1)} %param.12) | copy-start | bytes 1179652
  1.4 33.7 %copy-start.24 = (bf16[2,384]{1,0:T(2,128)(2,1)}, bf16[2,384]{1,0:T(2,128)(2,1)S(1)}, u32[]{:S(2)}) copy-start(bf16[2,384]{1,0:T(2,128)(2,1)S(1)} %fusion.57) | copy-start | bytes 4612
  2.7 34.4 %copy-start.21 = (f32[2,256]{1,0:T(2,128)}, f32[2,256]{1,0:T(2,128)S(1)}, u32[]{:S(2)}) copy-start(f32[2,256]{1,0:T(2,128)S(1)} %broadcast_multiply_fusion.5) | copy-start | bytes 6148
  3.9 33.1 %copy-start.31 = (f32[2,256]{1,0:T(2,128)}, f32[2,256]{1,0:T(2,128)S(1)}, u32[]{:S(2)}) copy-start(f32[2,256]{1,0:T(2,128)S(1)} %add_rsqrt_fusion.1) | copy-start | bytes 6148
  37.0 2.8 %copy-start.28 = (f32[2,384]{1,0:T(2,128)}, f32[2,384]{1,0:T(2,128)S(1)}, u32[]{:S(2)}) copy-start(f32[2,384]{1,0:T(2,128)S(1)} %get-tuple-element.68) | copy-start | bytes 9220
  46.0 2.2 %copy-start.27 = (f32[2,384]{1,0:T(2,128)S(1)}, f32[2,384]{1,0:T(2,128)}, u32[]{:S(2)}) copy-start(f32[2,384]{1,0:T(2,128)} %get-tuple-element.66) | copy-start | bytes 9220
  46.0 2.2 %copy-start.30 = (f32[1536]{0:T(1024)S(1)}, f32[1536]{0:T(1024)}, u32[]{:S(2)}) copy-start(f32[1536]{0:T(1024)} %slice.130) | copy-start | bytes 18436
  46.0 2.2 %copy-start.44 = (f32[2,384]{1,0:T(2,128)S(1)}, f32[2,384]{1,0:T(2,128)}, u32[]{:S(2)}) copy-start(f32[2,384]{1,0:T(2,128)} %get-tuple-element.65) | copy-start | bytes 9220
  49.4 2.5 %copy-start.49 = (bf16[4,384,384]{2,1,0:T(8,128)(2,1)S(1)}, bf16[4,384,384]{2,1,0:T(8,128)(2,1)}, u32[]{:S(2)}) copy-start(bf16[4,384,384]{2,1,0:T(8,128)(2,1)} %get-tuple-element.22) | copy-start | bytes 3538948
  80.2 2.2 %copy-start.38 = (bf16[1536]{0:T(1024)(128)(2,1)S(1)}, bf16[1536]{0:T(1024)(128)(2,1)}, u32[]{:S(2)}) copy-start(bf16[1536]{0:T(1024)(128)(2,1)} %get-tuple-element.80) | copy-start | bytes 9220
  80.3 2.4 %copy-start.36 = (bf16[384]{0:T(512)(128)(2,1)S(1)}, bf16[384]{0:T(512)(128)(2,1)}, u32[]{:S(2)}) copy-start(bf16[384]{0:T(512)(128)(2,1)} %get-tuple-element.59) | copy-start | bytes 2308
  81.2 2.1 %copy-start.29 = (f32[2,384]{1,0:T(2,128)S(1)}, f32[2,384]{1,0:T(2,128)}, u32[]{:S(2)}) copy-start(f32[2,384]{1,0:T(2,128)} %copy-done.28) | copy-start | bytes 9220
  81.2 2.1 %copy-start.32 = (f32[2,256]{1,0:T(2,128)S(1)}, f32[2,256]{1,0:T(2,128)}, u32[]{:S(2)}) copy-start(f32[2,256]{1,0:T(2,128)} %copy-done.31) | copy-start | bytes 6148
  83.4 2.3 %copy-start.43 = (f32[2,384]{1,0:T(2,128)S(1)}, f32[2,384]{1,0:T(2,128)}, u32[]{:S(2)}) copy-start(f32[2,384]{1,0:T(2,128)} %copy-done.42) | copy-start | bytes 9220
  89.2 2.2 %copy-start.6 = (f32[2,256,384]{2,1,0:T(8,128)S(1)}, f32[2,256,384]{2,1,0:T(8,128)}, u32[]{:S(2)}) copy-start(f32[2,256,384]{2,1,0:T(8,128)} %get-tuple-element.72) | copy-start | bytes 2359300
  89.2 2.2 %copy-start.7 = (f32[2,256,384]{2,1,0:T(8,128)S(1)}, f32[2,256,384]{2,1,0:T(8,128)}, u32[]{:S(2)}) copy-start(f32[2,256,384]{2,1,0:T(8,128)} %get-tuple-element.45) | copy-start | bytes 2359300
  92.5 57.1 %copy-start.35 = (bf16[2,384]{1,0:T(2,128)(2,1)S(1)}, bf16[2,384]{1,0:T(2,128)(2,1)}, u32[]{:S(2)}) copy-start(bf16[2,384]{1,0:T(2,128)(2,1)} %param.13) | copy-start | bytes 4612
  148.7 3.4 %copy-start.23 = (bf16[1344]{0:T(1024)(128)(2,1)S(1)}, bf16[1344]{0:T(1024)(128)(2,1)}, u32[]{:S(2)}) copy-start(bf16[1344]{0:T(1024)(128)(2,1)} %param.17) | copy-start | bytes 8068
  148.8 3.4 %copy-start.40 = (bf16[1344]{0:T(1024)(128)(2,1)S(1)}, bf16[1344]{0:T(1024)(128)(2,1)}, u32[]{:S(2)}) copy-start(bf16[1344]{0:T(1024)(128)(2,1)} %param.22) | copy-start | bytes 8068
  148.8 3.4 %copy-start.41 = (bf16[1344]{0:T(1024)(128)(2,1)S(1)}, bf16[1344]{0:T(1024)(128)(2,1)}, u32[]{:S(2)}) copy-start(bf16[1344]{0:T(1024)(128)(2,1)} %param.23) | copy-start | bytes 8068
  150.3 3.0 %copy-start.14 = (bf16[2,4,144,384]{3,2,1,0:T(8,128)(2,1)S(1)}, bf16[2,4,144,384]{3,2,1,0:T(8,128)(2,1)}, u32[]{:S(2)}) copy-start(bf16[2,4,144,384]{3,2,1,0:T(8,128)(2,1)} %get-tuple-element.25) | copy-start | bytes 2654212
  153.5 2.6 %copy-start.1 = (bf16[96,5376]{1,0:T(8,128)(2,1)S(1)}, bf16[96,5376]{1,0:T(8,128)(2,1)}, u32[]{:S(2)}) copy-start(bf16[96,5376]{1,0:T(8,128)(2,1)} %param.15) | copy-start | bytes 3096580
  153.5 2.5 %copy-start.12 = (bf16[96,5376]{1,0:T(8,128)(2,1)S(1)}, bf16[96,5376]{1,0:T(8,128)(2,1)}, u32[]{:S(2)}) copy-start(bf16[96,5376]{1,0:T(8,128)(2,1)} %param.18) | copy-start | bytes 3096580
  153.5 2.5 %copy-start.13 = (bf16[96,5376]{1,0:T(8,128)(2,1)S(1)}, bf16[96,5376]{1,0:T(8,128)(2,1)}, u32[]{:S(2)}) copy-start(bf16[96,5376]{1,0:T(8,128)(2,1)} %param.19) | copy-start | bytes 3096580
  (26 other events, 34.1 us)

commit v2 on v1

--- a/solution.py
+++ b/solution.py
@@ -1,3 +1,4 @@
+import math
 from functools import partial
 
 import jax
@@ -238,6 +239,224 @@
     )
 
 
+def dot(left, right, left_dim=1, right_dim=0):
+    return lax.dot_general(
+        left, right, (((left_dim,), (right_dim,)), ((), ())), preferred_element_type=jnp.float32
+    )
+
+
+def column_sum(values):
+    return jnp.sum(values, axis=0, keepdims=True)
+
+
+def feed_half(
+    token_ref, upstream_ref, mod_ref, bias_ref, rows_ref, down_ref,
+    out_ref, packed_ref, small,
+    input_one, projected, soft, mixed, input_two, active, delta_hidden, delta_feed,
+    delta_branch, delta_residual, delta_mixed,
+):
+    latents, positions, width = token_ref.shape
+    heads = width // HEAD
+
+    def one(latent, carry):
+        tokens = token_ref[latent].astype(jnp.float32)
+        upstream = upstream_ref[latent].astype(jnp.float32)
+        shift_one, scale_one, gate_one, shift_two, scale_two, gate_two = (
+            mod_ref[latent, at : at + 1] for at in range(6)
+        )
+        rows = pl.ds(pl.multiple_of(latent * positions, 16), positions)
+        normed_one, _ = normalize(tokens)
+        first_input = (normed_one * (1.0 + scale_one) + shift_one).astype(jnp.bfloat16)
+        input_one[rows] = first_input
+        for block in range(3):
+            cols = slice(block * width, (block + 1) * width)
+            value = dot(first_input, rows_ref[:, cols])
+            if block != 1:
+                value = value + bias_ref[block // 2 : block // 2 + 1]
+            projected[rows, cols] = value.astype(jnp.bfloat16)
+        for pair in range(heads // 2):
+            two = []
+            low = 2 * pair * HEAD
+            q2, k2, v2 = (
+                projected[rows, at * width + low : at * width + low + 2 * HEAD] for at in range(3)
+            )
+            for at in range(2):
+                here = slice(at * HEAD, (at + 1) * HEAD)
+                scores = dot(q2[:, here], k2[:, here], 1, 1) * HEAD ** (-0.5)
+                power = jnp.exp(scores - jnp.max(scores, axis=-1, keepdims=True))
+                weights = power * (1.0 / jnp.sum(power, axis=-1, keepdims=True))
+                soft[latent * heads + 2 * pair + at] = weights
+                two.append(dot(weights.astype(jnp.bfloat16), v2[:, here]))
+            mixed[rows, low : low + 2 * HEAD] = jnp.concatenate(two, axis=1).astype(jnp.bfloat16)
+        branch = dot(mixed[rows, :], rows_ref[:, 3 * width : 4 * width]) + bias_ref[2:3]
+        residual = tokens + gate_one * branch
+        normed_two, inv_two = normalize(residual)
+        second_input = (normed_two * (1.0 + scale_two) + shift_two).astype(jnp.bfloat16)
+        input_two[rows] = second_input
+        feed_delta = (gate_two * upstream).astype(jnp.bfloat16)
+        delta_feed[rows] = feed_delta
+        small[23:24] += column_sum(feed_delta.astype(jnp.float32))
+        feed_out = jnp.zeros((positions, width), jnp.float32) + bias_ref[7:8]
+        delta_input = jnp.zeros((positions, width), jnp.float32)
+        root = math.sqrt(2.0 / math.pi)
+        for block in range(4):
+            cols = slice(block * width, (block + 1) * width)
+            expand = rows_ref[:, (4 + block) * width : (5 + block) * width]
+            hidden = dot(second_input, expand) + bias_ref[3 + block : 4 + block]
+            square = hidden * hidden
+            bend = jnp.tanh(root * hidden * (1.0 + 0.044715 * square))
+            half = 0.5 + 0.5 * bend
+            low_active = (hidden * half).astype(jnp.bfloat16)
+            slope = half + hidden * (0.5 * root) * (1.0 - bend * bend) * (
+                1.0 + (3.0 * 0.044715) * square
+            )
+            active[rows, cols] = low_active
+            feed_out = feed_out + dot(low_active, down_ref[cols, :])
+            low_delta = (dot(feed_delta, down_ref[cols, :], 1, 1) * slope).astype(jnp.bfloat16)
+            delta_hidden[rows, cols] = low_delta
+            small[19 + block : 20 + block] += column_sum(low_delta.astype(jnp.float32))
+            delta_input = delta_input + dot(low_delta, expand, 1, 1)
+        out_ref[latent] = (residual + gate_two * feed_out).astype(jnp.bfloat16)
+        residual_delta = upstream + norm_back(delta_input * (1.0 + scale_two), normed_two, inv_two)
+        delta_residual[rows] = residual_delta
+        branch_delta = (gate_one * residual_delta).astype(jnp.bfloat16)
+        delta_branch[rows] = branch_delta
+        small[18:19] += column_sum(branch_delta.astype(jnp.float32))
+        delta_mixed[rows] = dot(branch_delta, rows_ref[:, 3 * width : 4 * width], 1, 1).astype(
+            jnp.bfloat16
+        )
+        small[pl.ds(latent * 6 + 2, 1)] = column_sum(residual_delta * branch)
+        small[pl.ds(latent * 6 + 3, 1)] = column_sum(delta_input)
+        small[pl.ds(latent * 6 + 4, 1)] = column_sum(delta_input * normed_two)
+        small[pl.ds(latent * 6 + 5, 1)] = column_sum(upstream * feed_out)
+        return carry
+
+    lax.fori_loop(0, latents, one, 0)
+    own_rows = width // 4
+    for block in range(4):
+        cols = slice(block * width, (block + 1) * width)
+        total = dot(active[:, cols], delta_feed[...], 0, 0).astype(jnp.bfloat16)
+        packed_ref[block, 8 * own_rows :] = total
+        put_block(packed_ref, 4 + block, dot(input_two[...], delta_hidden[:, cols], 0, 0))
+    put_block(packed_ref, 3, dot(mixed[...], delta_branch[...], 0, 0))
+
+
+def put_block(packed_ref, block, total):
+    own_rows = total.shape[0] // 4
+    for shard in range(4):
+        packed_ref[shard, block * own_rows : (block + 1) * own_rows] = total[
+            shard * own_rows : (shard + 1) * own_rows
+        ].astype(jnp.bfloat16)
+
+
+def attention_half(
+    token_ref, mod_ref, rows_ref, grad_ref, packed_ref, small,
+    input_one, projected, soft, delta_residual, delta_mixed, delta_projected,
+):
+    latents, positions, width = token_ref.shape
+    heads = width // HEAD
+
+    def one(latent, carry):
+        scale_one = mod_ref[latent, 1:2]
+        rows = pl.ds(pl.multiple_of(latent * positions, 16), positions)
+        for pair in range(heads // 2):
+            low = 2 * pair * HEAD
+            q2, k2, v2 = (
+                projected[rows, at * width + low : at * width + low + 2 * HEAD] for at in range(3)
+            )
+            m2 = delta_mixed[rows, low : low + 2 * HEAD]
+            found = ([], [], [])
+            for at in range(2):
+                here = slice(at * HEAD, (at + 1) * HEAD)
+                weights = soft[latent * heads + 2 * pair + at]
+                delta_soft = dot(m2[:, here], v2[:, here], 1, 1)
+                inner = jnp.sum(delta_soft * weights, axis=-1, keepdims=True)
+                delta_scores = (weights * (delta_soft - inner)).astype(jnp.bfloat16)
+                found[0].append(dot(delta_scores, k2[:, here]) * HEAD ** (-0.5))
+                found[1].append(dot(delta_scores, q2[:, here], 0, 0) * HEAD ** (-0.5))
+                found[2].append(dot(weights.astype(jnp.bfloat16), m2[:, here], 0, 0))
+            for at in range(3):
+                delta_projected[rows, at * width + low : at * width + low + 2 * HEAD] = (
+                    jnp.concatenate(found[at], axis=1).astype(jnp.bfloat16)
+                )
+        small[16:17] += column_sum(delta_projected[rows, :width].astype(jnp.float32))
+        small[17:18] += column_sum(delta_projected[rows, 2 * width :].astype(jnp.float32))
+        delta_input = dot(delta_projected[rows, :], rows_ref[:, : 3 * width], 1, 1)
+        normed_one, inv_one = normalize(token_ref[latent].astype(jnp.float32))
+        grad_ref[latent] = (
+            delta_residual[rows, :]
+            + norm_back(delta_input * (1.0 + scale_one), normed_one, inv_one)
+        ).astype(jnp.bfloat16)
+        small[pl.ds(latent * 6, 1)] = column_sum(delta_input)
+        small[pl.ds(latent * 6 + 1, 1)] = column_sum(delta_input * normed_one)
+        return carry
+
+    lax.fori_loop(0, latents, one, 0)
+    for block in range(3):
+        put_block(
+            packed_ref,
+            block,
+            dot(input_one[...], delta_projected[:, block * width : (block + 1) * width], 0, 0),
+        )
+
+
+def block_kernel(
+    token_ref, upstream_ref, mod_ref, bias_ref, rows_ref, down_ref, silu_ref,
+    out_ref, grad_ref, packed_ref, small_ref,
+    small, input_one, projected, soft, mixed, input_two, active, delta_hidden, delta_feed,
+    delta_branch, delta_residual, delta_mixed, delta_projected,
+):
+    small[...] = jnp.zeros_like(small)
+    small[12:14] = silu_ref[...].astype(jnp.float32)
+    feed_half(
+        token_ref, upstream_ref, mod_ref, bias_ref, rows_ref, down_ref,
+        out_ref, packed_ref, small,
+        input_one, projected, soft, mixed, input_two, active, delta_hidden, delta_feed,
+        delta_branch, delta_residual, delta_mixed,
+    )
+    attention_half(
+        token_ref, mod_ref, rows_ref, grad_ref, packed_ref, small,
+        input_one, projected, soft, delta_residual, delta_mixed, delta_projected,
+    )
+    small_ref[...] = small[...].astype(jnp.bfloat16)
+
+
+def block_gradients(tokens, cotangent, modulation, biases, rows_full, down_full, silu_cond):
+    latents, positions, width = tokens.shape
+    count, hidden_width = latents * positions, down_full.shape[0]
+    own_rows = width // 4
+    bf16, f32 = jnp.bfloat16, jnp.float32
+    vmem = pl.BlockSpec(memory_space=pltpu.VMEM)
+    return pl.pallas_call(
+        block_kernel,
+        out_shape=(
+            jax.ShapeDtypeStruct(tokens.shape, bf16),
+            jax.ShapeDtypeStruct(tokens.shape, bf16),
+            jax.ShapeDtypeStruct((4, 8 * own_rows + hidden_width // 4, width), bf16),
+            jax.ShapeDtypeStruct((32, width), bf16),
+        ),
+        in_specs=[vmem] * 7,
+        out_specs=(vmem,) * 4,
+        scratch_shapes=[
+            pltpu.VMEM((32, width), f32),
+            pltpu.VMEM((count, width), bf16),
+            pltpu.VMEM((count, 3 * width), bf16),
+            pltpu.VMEM((latents * HEADS, positions, positions), f32),
+            pltpu.VMEM((count, width), bf16),
+            pltpu.VMEM((count, width), bf16),
+            pltpu.VMEM((count, hidden_width), bf16),
+            pltpu.VMEM((count, hidden_width), bf16),
+            pltpu.VMEM((count, width), bf16),
+            pltpu.VMEM((count, width), bf16),
+            pltpu.VMEM((count, width), f32),
+            pltpu.VMEM((count, width), bf16),
+            pltpu.VMEM((count, 3 * width), bf16),
+        ],
+        compiler_params=pltpu.CompilerParams(vmem_limit_bytes=VMEM_BYTES),
+        name="block_gradients",
+    )(tokens, cotangent, modulation, biases, rows_full, down_full, silu_cond)
+
+
 def reduce_kernel(
     packed_ref,
     small_ref,
@@ -429,10 +648,13 @@
 
 
 def reduce_gradients(
-    packed, delta_modulation, silu_cond, bias_local, w_rows, shards, replicas
+    packed, small, w_rows, latents, shards, replicas
 ):
-    latents, width = silu_cond.shape
+    width = packed.shape[-1]
     own_rows, six_width = w_rows.shape[0], 6 * width
+    delta_modulation = small[: 6 * latents].reshape(latents, six_width)
+    silu_cond = small[6 * latents : 7 * latents]
+    bias_local = small[16:24].astype(jnp.float32).reshape(-1)
     if shards != 4 or replicas != 8 or latents != 2:
         summed = lax.psum_scatter(
             packed.reshape(-1, width).astype(jnp.float32), "shard", scatter_dimension=0, tiled=True
@@ -448,16 +670,6 @@
             matrix_multiply("le,de->ld", delta_modulation, cond_matrix),
         )
     whole = packed.shape[1]
-    small = jnp.concatenate(
-        [
-            delta_modulation.reshape(6 * latents, width),
-            silu_cond,
-            jnp.zeros((16 - 7 * latents, width), jnp.bfloat16),
-            bias_local.astype(jnp.bfloat16).reshape(-1, width),
-            jnp.zeros((16 - bias_local.shape[0] // width, width), jnp.bfloat16),
-        ],
-        axis=0,
-    )
     vmem = pl.BlockSpec(memory_space=pltpu.VMEM)
     bf16 = jnp.bfloat16
     summed, every, silu_parts = pl.pallas_call(
@@ -516,7 +728,6 @@
     bias_second,
 ):
     latents, positions, embedding_width = tokens.shape
-    hidden_units_width = w_rows.shape[1] - 10 * embedding_width
     six_width = 6 * embedding_width
     cond_values = condition.astype(jnp.float32)
     silu_cond = jax.nn.silu(cond_values).astype(jnp.bfloat16)
@@ -525,145 +736,23 @@
     )
     bias_entries = bias_full.astype(jnp.float32)
     modulation = modulation + bias_entries[:six_width]
-    triple_matrix = rows_full[:, : 3 * embedding_width]
-    output_matrix = rows_full[:, 3 * embedding_width : 4 * embedding_width]
-    expand_weight = rows_full[:, 4 * embedding_width :]
-    blocks_six = [
-        modulation[:, None, index * embedding_width : (index + 1) * embedding_width]
-        for index in range(6)
-    ]
-    shift_attention, scale_attention, gate_attention, shift_feed, scale_feed, gate_feed = blocks_six
-    token_values = tokens.astype(jnp.float32)
-    normed_attention, inv_attention = normalize(token_values)
-    input_attention = (normed_attention * (1.0 + scale_attention) + shift_attention).astype(
-        jnp.bfloat16
-    )
-    zeros_key = jnp.zeros((embedding_width,), jnp.float32)
-    triple_bias = jnp.concatenate(
-        [
-            bias_entries[six_width : 7 * embedding_width],
-            zeros_key,
-            bias_entries[7 * embedding_width : 8 * embedding_width],
-        ]
-    )
-    projected = (
-        matrix_multiply("lsd,de->lse", input_attention, triple_matrix) + triple_bias
-    ).astype(jnp.bfloat16)
-    head_shape = (latents, positions, HEADS, HEAD)
-    flat_shape = (latents, positions, embedding_width)
-    query = projected[..., :embedding_width].reshape(head_shape)
-    keys = projected[..., embedding_width : 2 * embedding_width].reshape(head_shape)
-    values = projected[..., 2 * embedding_width :].reshape(head_shape)
-    score_scale = HEAD ** (-0.5)
-    scores = matrix_multiply("lqhe,lkhe->lhqk", query, keys) * score_scale
-    log_total = jax.nn.logsumexp(scores, axis=-1, keepdims=True)
-    softmax_low = jnp.exp(scores - log_total).astype(jnp.bfloat16)
-    mixed_heads = (
-        matrix_multiply("lhqk,lkhe->lqhe", softmax_low, values)
-        .reshape(flat_shape)
-        .astype(jnp.bfloat16)
-    )
-    branch = (
-        matrix_multiply("lsd,de->lse", mixed_heads, output_matrix)
-        + bias_entries[8 * embedding_width : 9 * embedding_width]
-    )
-    residual = token_values + gate_attention * branch
-    normed_feed, inv_feed = normalize(residual)
-    feed_input = (normed_feed * (1.0 + scale_feed) + shift_feed).astype(jnp.bfloat16)
-    hidden = (
-        matrix_multiply("wqg,gc->wqc", feed_input, expand_weight)
-        + bias_entries[9 * embedding_width : 9 * embedding_width + hidden_units_width]
-    )
-    gelu_out, gelu_pull = jax.vjp(partial(jax.nn.gelu, approximate=True), hidden)
-    activated_hidden = gelu_out.astype(jnp.bfloat16)
-    feed_out = (
-        matrix_multiply("wku,ux->wkx", activated_hidden, shrink_weight)
-        + bias_entries[9 * embedding_width + hidden_units_width :]
-    )
-    block_out = (residual + gate_feed * feed_out).astype(jnp.bfloat16)
-    upstream = cotangent.astype(jnp.float32)
-    delta_gate_feed = jnp.sum(upstream * feed_out, axis=1)
-    delta_feed_branch = (gate_feed * upstream).astype(jnp.bfloat16)
-    summed_down_weight = matrix_multiply("pxz,pxk->zk", activated_hidden, delta_feed_branch)
-    bias_down = jnp.sum(delta_feed_branch.astype(jnp.float32), axis=(0, 1))
-    delta_activated = matrix_multiply("tgw,uw->tgu", delta_feed_branch, shrink_weight)
-    delta_hidden_units = gelu_pull(delta_activated)[0].astype(jnp.bfloat16)
-    summed_expand_weight = matrix_multiply("pce,pcw->ew", feed_input, delta_hidden_units)
-    bias_expand = jnp.sum(delta_hidden_units.astype(jnp.float32), axis=(0, 1))
-    delta_feed_input = matrix_multiply("kzq,wq->kzw", delta_hidden_units, expand_weight)
-    delta_shift_feed = jnp.sum(delta_feed_input, axis=1)
-    delta_scale_feed = jnp.sum(delta_feed_input * normed_feed, axis=1)
-    delta_residual = upstream + norm_back(
-        delta_feed_input * (1.0 + scale_feed), normed_feed, inv_feed
-    )
-    delta_gate_attention = jnp.sum(delta_residual * branch, axis=1)
-    delta_branch = (gate_attention * delta_residual).astype(jnp.bfloat16)
-    total_output = matrix_multiply("lsd,lse->de", mixed_heads, delta_branch)
-    bias_output = jnp.sum(delta_branch.astype(jnp.float32), axis=(0, 1))
-    delta_mixed = (
-        matrix_multiply("lse,de->lsd", delta_branch, output_matrix)
-        .astype(jnp.bfloat16)
-        .reshape(head_shape)
-    )
-    scores_again = matrix_multiply("lqhe,lkhe->lhqk", query, keys) * score_scale
-    softmax_full = jnp.exp(scores_again - log_total)
-    softmax_again = softmax_full.astype(jnp.bfloat16)
-    delta_soft = matrix_multiply("lqhe,lkhe->lhqk", delta_mixed, values)
-    delta_values = matrix_multiply("lhqk,lqhe->lkhe", softmax_again, delta_mixed).astype(
-        jnp.bfloat16
-    )
-    row_inner = jnp.sum(delta_soft * softmax_full, axis=-1, keepdims=True)
-    delta_scores = (softmax_full * (delta_soft - row_inner)).astype(jnp.bfloat16)
-    delta_query = (matrix_multiply("lhqk,lkhe->lqhe", delta_scores, keys) * score_scale).astype(
-        jnp.bfloat16
-    )
-    delta_keys = (matrix_multiply("lhqk,lqhe->lkhe", delta_scores, query) * score_scale).astype(
-        jnp.bfloat16
-    )
-    delta_projected = jnp.concatenate(
-        [
-            delta_query.reshape(flat_shape),
-            delta_keys.reshape(flat_shape),
-            delta_values.reshape(flat_shape),
-        ],
-        axis=-1,
-    )
-    total_triple = matrix_multiply("lsd,lse->de", input_attention, delta_projected)
-    bias_query = jnp.sum(delta_query.reshape(flat_shape).astype(jnp.float32), axis=(0, 1))
-    bias_valued = jnp.sum(delta_values.reshape(flat_shape).astype(jnp.float32), axis=(0, 1))
-    delta_input_attention = matrix_multiply("lse,de->lsd", delta_projected, triple_matrix)
-    delta_shift_attention = jnp.sum(delta_input_attention, axis=1)
-    delta_scale_attention = jnp.sum(delta_input_attention * normed_attention, axis=1)
-    delta_tokens = delta_residual + norm_back(
-        delta_input_attention * (1.0 + scale_attention), normed_attention, inv_attention
-    )
-    tokens_grad = delta_tokens.astype(jnp.bfloat16)
-    delta_modulation = jnp.concatenate(
-        [
-            delta_shift_attention,
-            delta_scale_attention,
-            delta_gate_attention,
-            delta_shift_feed,
-            delta_scale_feed,
-            delta_gate_feed,
-        ],
-        axis=1,
-    ).astype(jnp.bfloat16)
-    bias_local = jnp.concatenate([bias_query, bias_valued, bias_output, bias_expand, bias_down])
-    total_rows = jnp.concatenate([total_triple, total_output, summed_expand_weight], axis=1)
-    blocks = total_rows.shape[1] // embedding_width
+    modulation = jnp.pad(
+        modulation.reshape(latents, 6, embedding_width), ((0, 0), (0, 2), (0, 0))
+    )
+    block_out, tokens_grad, packed, small = block_gradients(
+        tokens,
+        cotangent,
+        modulation,
+        bias_entries[six_width:].reshape(-1, embedding_width),
+        rows_full,
+        shrink_weight,
+        silu_cond,
+    )
+    summed, every_modulation, every_silu, bias_rest, delta_silu = reduce_gradients(
+        packed, small, w_rows, latents, shards, replicas
+    )
+    blocks = rows_full.shape[1] // embedding_width
     shard_rows = w_rows.shape[0]
-    packed_rows = (
-        total_rows.astype(jnp.bfloat16)
-        .reshape(shards, shard_rows, blocks, embedding_width)
-        .transpose(0, 2, 1, 3)
-        .reshape(shards, blocks * shard_rows, embedding_width)
-    )
-    packed_down = summed_down_weight.astype(jnp.bfloat16).reshape(shards, -1, embedding_width)
-    packed = jnp.concatenate([packed_rows, packed_down], axis=1)
-    summed, every_modulation, every_silu, bias_rest, delta_silu = reduce_gradients(
-        packed, delta_modulation, silu_cond, bias_local, w_rows, shards, replicas
-    )
     shard_at = lax.axis_index("shard")
     own_silu = lax.dynamic_slice_in_dim(every_silu, shard_at * shard_rows, shard_rows, 1)
     total_cond = matrix_multiply("ld,le->de", own_silu, every_modulation)

time: 161 us -> 122 us (0.76)
  matrix products: 31.6 us -> 0.39 us
  Pallas kernels: 77 us -> 102 us
  local copies, waits for them, and re-layouts: 32.1 us -> 11.4 us
  other arithmetic: 17.7 us -> 7.52 us
    dot_general x19 -> x1, matrix products: 31.6 us -> 0.39 us  [matrix_multiply(): jnp.einsum(spec_text, left, right, preferred_element_type=jnp.float32)]
    pallas_call x0 -> x1, Pallas kernels: none -> 24.8 us  [block_gradients(): pl.pallas_call(block_kernel, out_shape=(jax.ShapeDtypeStruct(tokens.shape...]
    reduce_sum x6 -> x0, other arithmetic: 6.35 us -> none  [the longest x1 1.95 us: per_device(): bias_output = jnp.sum(delta_branch.astype(jnp.float32), axis=(0, 1))]
    unnamed x111 -> x27, local copies, waits for them, and re-layouts: 7.49 us -> 2.4 us
    slice x6 -> x1, local copies, waits for them, and re-layouts: 4.09 us -> 0.6 us  [per_device(): bias_entries[six_width:].reshape(-1, embedding_width)]
    concatenate x3 -> x0, local copies, waits for them, and re-layouts: 3.33 us -> none  [the longest x1 3.11 us: reduce_gradients(): jnp.concatenate([delta_modulation.reshape(6 * latents, width), silu_cond,...]
    concatenate x3 -> x0, other arithmetic: 2.43 us -> none  [the longest x1 2.11 us: per_device(): packed = jnp.concatenate([packed_rows, packed_down], axis=1)]
    reshape x3 -> x0, local copies, waits for them, and re-layouts: 2.34 us -> none  [the longest x1 1.92 us: per_device(): delta_values.reshape(flat_shape)]
where the time goes in v2:
time: 122 us
  Pallas kernels  102 us (84%)
  local copies, waits for them, and re-layouts  11.4 us (9%)
  other arithmetic  7.52 us (6%)
    pallas_call x1, Pallas kernels, reduce_gradients(): pl.pallas_call(reduce_kernel, out_shape=(jax.ShapeDtypeStruct((2, 4, whol...  52.9 us
    pallas_call x1, Pallas kernels, block_gradients(): pl.pallas_call(block_kernel, out_shape=(jax.ShapeDtypeStruct(tokens.shape...  24.8 us
    pallas_call x1, Pallas kernels, gather_weights(): pl.pallas_call(gather_kernel, out_shape=(jax.ShapeDtypeStruct((shards,) +...  24.1 us
    sub x3, other arithmetic, adam_step(): master - learn_rate * (first_hat / (jnp.sqrt(second_hat) + adam_eps) + we...  6.02 us

profile of v2, /device:TPU:0, one launch (start us, length us, event | category | flops | bytes accessed | tf_op | source)
XLA Modules:
  0.0 122.0 jit_solution(11801376237107987652)
XLA Ops:
  0.7 1.8 %slice.40.cond_ref = bf16[96,2304]{1,0:T(8,128)(2,1)} slice(bf16[96,5376]{1,0:T(8,128)(2,1)} %param.15), slice={[0:96], [0:2304]} | slice | bytes 884736 | tf_op jit(solution)/shard_map/slice | solution.py:232
  2.5 0.7 fusion.16.silu_ref
  3.3 0.6 pad.13.silu_ref
  3.9 1.9 %slice.39.rows_ref = bf16[96,3072]{1,0:T(8,128)(2,1)} slice(bf16[96,5376]{1,0:T(8,128)(2,1)} %param.15), slice={[0:96], [2304:5376]} | slice | bytes 1179648 | tf_op jit(solution)/shard_map/slice | solution.py:208
  5.8 0.6 pad_bitcast_fusion.bias_ref
  6.4 24.1 %gather_weights.1 = (bf16[4,96,3072]{2,1,0:T(8,128)(2,1)}, bf16[4,384,384]{2,1,0:T(8,128)(2,1)}, bf16[4,16,128]{2,1,0:T(8,128)(2,1)}, f32[16,384]{1,0:T(8,128)}) custom-call(bf16[96,3072]{1,0:T(8,128)(2,1)} %slice.39.rows_ref, bf16[384,384]{1,0:T(8,128)(2,1)} %down_ref.1, bf16[16,128]{1,0:T(8,128)(2,1)} %pad_bitcast_fusion.bias_ref, ...), custom_call_target="tpu_custom_call" | custom-call | tf_op jit(solution)/shard_map/gather_weights/pallas_call | solution.py:210
  30.5 0.7 copy.33
  31.2 0.1 reshape.102
  31.3 0.7 reshape.91
  32.1 0.6 pad.14.mod_ref
  32.7 0.6 slice.53.bias_ref
  33.3 24.8 %block_gradients.1 = (bf16[2,256,384]{2,1,0:T(8,128)(2,1)}, bf16[2,256,384]{2,1,0:T(8,128)(2,1)}, bf16[4,1152,384]{2,1,0:T(8,128)(2,1)}, bf16[32,384]{1,0:T(8,128)(2,1)}) custom-call(bf16[2,256,384]{2,1,0:T(8,128)(2,1)} %token_ref.1, bf16[2,256,384]{2,1,0:T(8,128)(2,1)} %upstream_ref.1, f32[2,8,384]{2,1,0:T(8,128)} %pad.14.mod_ref, ...), custom_call_target="tpu_custom_call" | custom-call | tf_op jit(solution)/shard_map/block_gradients/pallas_call | solution.py:430
  58.1 52.9 %reduce_gradients.1 = (bf16[2,4,144,384]{3,2,1,0:T(8,128)(2,1)}, bf16[4,2,4,32,384]{4,3,2,1,0:T(8,128)(2,1)}, f32[4,16,128]{2,1,0:T(8,128)}) custom-call(bf16[4,1152,384]{2,1,0:T(8,128)(2,1)} %get-tuple-element.29.packed_ref, bf16[32,384]{1,0:T(8,128)(2,1)} %get-tuple-element.30.small_ref, bf16[96,2304]{1,0:T(8,128)(2,1)} %slice.40.cond_ref), custom_call_target="tpu_custom_call" | custom-call | tf_op jit(solution)/shard_map/reduce_gradients/pallas_call | solution.py:675
  111.0 1.3 %copy.28 = bf16[4,4,2,32,384]{4,3,2,1,0:T(8,128)(2,1)S(1)} copy(bf16[4,4,2,32,384]{4,3,1,2,0:T(8,128)(2,1)} %bitcast.33) | data formatting | bytes 1572864 | tf_op jit(solution)/shard_map/transpose | solution.py:701
  112.3 0.3 reshape.99
  112.8 0.7 convert_subtract_fusion.2
  113.6 0.4 fusion.7
  114.2 0.1 copy.30
  114.3 1.0 copy-done
  115.3 0.3 copy-done.2
  115.6 0.3 copy-done.3
  115.9 3.8 %convert_subtract_fusion = (f32[96,5376]{1,0:T(8,128)}, f32[96,5376]{1,0:T(8,128)}, f32[96,5376]{1,0:T(8,128)}) fusion(bf16[96,5376]{1,0:T(8,128)(2,1)S(1)} %copy-done, f32[96,3072]{1,0:T(8,128)S(1)} %bitcast.24, f32[96,2304]{1,0:T(8,128)S(1)} %fusion.7, bf16[96,5376]{1,0:T(8,128)(2,1)S(1)} %copy-done.2, bf16[96,5376]{1,0:T(8,128)(2,1)S(1)} %copy-done.3), kind=kLoop, calls=%fused_computation.1 | loop fusion | flops 9805824 | bytes 11354112 | tf_op jit(solution)/shard_map/sub | solution.py:50
  119.7 1.5 %convert_subtract_fusion.1 = (f32[384,384]{1,0:T(8,128)}, f32[384,384]{1,0:T(8,128)}, f32[384,384]{1,0:T(8,128)}) fusion(bf16[384,384]{1,0:T(8,128)(2,1)S(1)} %copy-done.1, bf16[1152,384]{1,0:T(8,128)(2,1)S(1)} %bitcast.32, bf16[384,384]{1,0:T(8,128)(2,1)S(1)} %copy-done.5, bf16[384,384]{1,0:T(8,128)(2,1)S(1)} %copy-done.6), kind=kLoop, calls=%fused_computation.11 | loop fusion | flops 2801664 | bytes 2949120 | tf_op jit(solution)/shard_map/sub | solution.py:50
  121.4 0.6 fusion.18
  (40 shorter events, 0.7 us)
Async XLA Ops:
  0.6 5.2 %copy-start.8 = (bf16[1344]{0:T(1024)(128)(2,1)S(1)}, bf16[1344]{0:T(1024)(128)(2,1)}, u32[]{:S(2)}) copy-start(bf16[1344]{0:T(1024)(128)(2,1)} %param.17) | copy-start | bytes 8068
  3.2 30.1 %copy-start.9 = (bf16[2,384]{1,0:T(2,128)(2,1)}, bf16[2,384]{1,0:T(2,128)(2,1)S(1)}, u32[]{:S(2)}) copy-start(bf16[2,384]{1,0:T(2,128)(2,1)S(1)} %fusion.16.silu_ref) | copy-start | bytes 4612
  111.0 1.8 %copy-start.11 = (bf16[1344]{0:T(1024)(128)(2,1)S(1)}, bf16[1344]{0:T(1024)(128)(2,1)}, u32[]{:S(2)}) copy-start(bf16[1344]{0:T(1024)(128)(2,1)} %param.22) | copy-start | bytes 8068
  111.0 1.8 %copy-start.12 = (bf16[1344]{0:T(1024)(128)(2,1)S(1)}, bf16[1344]{0:T(1024)(128)(2,1)}, u32[]{:S(2)}) copy-start(bf16[1344]{0:T(1024)(128)(2,1)} %param.23) | copy-start | bytes 8068
  112.3 1.7 %copy-start.4 = (bf16[2,4,144,384]{3,2,1,0:T(8,128)(2,1)S(1)}, bf16[2,4,144,384]{3,2,1,0:T(8,128)(2,1)}, u32[]{:S(2)}) copy-start(bf16[2,4,144,384]{3,2,1,0:T(8,128)(2,1)} %get-tuple-element.33) | copy-start | bytes 2654212
  114.0 1.2 %copy-start = (bf16[96,5376]{1,0:T(8,128)(2,1)S(1)}, bf16[96,5376]{1,0:T(8,128)(2,1)}, u32[]{:S(2)}) copy-start(bf16[96,5376]{1,0:T(8,128)(2,1)} %param.15) | copy-start | bytes 3096580
  114.1 1.5 %copy-start.2 = (bf16[96,5376]{1,0:T(8,128)(2,1)S(1)}, bf16[96,5376]{1,0:T(8,128)(2,1)}, u32[]{:S(2)}) copy-start(bf16[96,5376]{1,0:T(8,128)(2,1)} %param.18) | copy-start | bytes 3096580
  114.1 1.8 %copy-start.3 = (bf16[96,5376]{1,0:T(8,128)(2,1)S(1)}, bf16[96,5376]{1,0:T(8,128)(2,1)}, u32[]{:S(2)}) copy-start(bf16[96,5376]{1,0:T(8,128)(2,1)} %param.19) | copy-start | bytes 3096580
  115.9 3.8 %copy-start.1 = (bf16[384,384]{1,0:T(8,128)(2,1)S(1)}, bf16[384,384]{1,0:T(8,128)(2,1)}, u32[]{:S(2)}) copy-start(bf16[384,384]{1,0:T(8,128)(2,1)} %down_ref.1) | copy-start | bytes 884740
  115.9 3.8 %copy-start.5 = (bf16[384,384]{1,0:T(8,128)(2,1)S(1)}, bf16[384,384]{1,0:T(8,128)(2,1)}, u32[]{:S(2)}) copy-start(bf16[384,384]{1,0:T(8,128)(2,1)} %param.20) | copy-start | bytes 884740
  115.9 3.8 %copy-start.6 = (bf16[384,384]{1,0:T(8,128)(2,1)S(1)}, bf16[384,384]{1,0:T(8,128)(2,1)}, u32[]{:S(2)}) copy-start(bf16[384,384]{1,0:T(8,128)(2,1)} %param.21) | copy-start | bytes 884740
  119.7 1.6 %copy-start.7 = (f32[4,16,128]{2,1,0:T(8,128)S(1)}, f32[4,16,128]{2,1,0:T(8,128)}, u32[]{:S(2)}) copy-start(f32[4,16,128]{2,1,0:T(8,128)} %get-tuple-element.31) | copy-start | bytes 98308
  119.7 1.7 %copy-start.10 = (bf16[2,384]{1,0:T(2,128)(2,1)S(1)}, bf16[2,384]{1,0:T(2,128)(2,1)}, u32[]{:S(2)}) copy-start(bf16[2,384]{1,0:T(2,128)(2,1)} %param.13) | copy-start | bytes 4612

commit v3 on v2

--- a/solution.py
+++ b/solution.py
@@ -96,7 +96,6 @@
     rows_ref,
     down_ref,
     bias_ref,
-    cond_ref,
     silu_ref,
     rows_out,
     down_out,
@@ -116,7 +115,10 @@
     meet([core, across, corner, beside])
     copies = Copies(send_sem, recv_sem)
     far = across[0]
-    columns = rows_ref.shape[1]
+    skip = 6 * mod_out.shape[1]
+    columns = rows_ref.shape[1] - skip
+    kept = rows_ref.at[:, pl.ds(skip, columns)]
+    cond_ref = rows_ref
     half_rows, half_down = rows_ref.shape[0] // 2, down_ref.shape[0] // 2
 
     silu_copies = [
@@ -129,7 +131,8 @@
         found = []
         for at in range(2):
             cols = pl.ds(at * (columns // 2), columns // 2)
-            found.append((rows_ref.at[low, cols], rows_out.at[slot, low, cols]))
+            from_cols = pl.ds(skip + at * (columns // 2), columns // 2)
+            found.append((rows_ref.at[low, from_cols], rows_out.at[slot, low, cols]))
         found.append((down_ref.at[low_down], down_out.at[slot, low_down]))
         return found
 
@@ -137,12 +140,12 @@
     first = [copies.start(source, target, across) for source, target in pieces(s, x)]
     near = [
         copies.start(bias_ref, bias_out.at[s], core),
-        copies.start(rows_ref, rows_out.at[s], core),
+        copies.start(kept, rows_out.at[s], core),
         copies.start(down_ref, down_out.at[s], core),
     ]
     own = [
         pltpu.make_async_copy(bias_ref, bias_out.at[s], own_sem.at[0]),
-        pltpu.make_async_copy(rows_ref, rows_out.at[s], own_sem.at[1]),
+        pltpu.make_async_copy(kept, rows_out.at[s], own_sem.at[1]),
         pltpu.make_async_copy(down_ref, down_out.at[s], own_sem.at[2]),
     ]
     for copy in own:
@@ -205,17 +208,17 @@
     spread = jnp.repeat(spread, 6, axis=1)
     spread = jnp.pad(spread, ((0, 0), (0, 16 - 6 * latents), (0, 128 - own_rows)))
     bias_tile = jnp.pad(bias_pack, (0, 2048 - bias_pack.shape[0])).reshape(16, 128)
-    rows = w_rows[:, six_width:]
+    columns = w_rows.shape[1] - six_width
     vmem = pl.BlockSpec(memory_space=pltpu.VMEM)
     rows_full, down_full, bias_full, mod = pl.pallas_call(
         gather_kernel,
         out_shape=(
-            jax.ShapeDtypeStruct((shards,) + rows.shape, jnp.bfloat16),
+            jax.ShapeDtypeStruct((shards, own_rows, columns), jnp.bfloat16),
             jax.ShapeDtypeStruct((shards,) + w_down.shape, jnp.bfloat16),
             jax.ShapeDtypeStruct((shards, 16, 128), jnp.bfloat16),
             jax.ShapeDtypeStruct((16, width), jnp.float32),
         ),
-        in_specs=[vmem] * 5,
+        in_specs=[vmem] * 4,
         out_specs=(vmem,) * 4,
         scratch_shapes=[
             pltpu.VMEM((shards, 16, 128), jnp.bfloat16),
@@ -229,10 +232,10 @@
             collective_id=0, has_side_effects=True, vmem_limit_bytes=VMEM_BYTES
         ),
         name="gather_weights",
-    )(rows, w_down, bias_tile, w_rows[:, :six_width], spread)
+    )(w_rows, w_down, bias_tile, spread)
     bias_full = bias_full.reshape(shards, 2048)[:, : bias_pack.shape[0]].reshape(-1)
     return (
-        rows_full.reshape(-1, rows.shape[1]),
+        rows_full.reshape(-1, columns),
         down_full.reshape(-1, width),
         bias_full,
         mod[: 6 * latents].reshape(latents, six_width),
@@ -338,7 +341,6 @@
         total = dot(active[:, cols], delta_feed[...], 0, 0).astype(jnp.bfloat16)
         packed_ref[block, 8 * own_rows :] = total
         put_block(packed_ref, 4 + block, dot(input_two[...], delta_hidden[:, cols], 0, 0))
-    put_block(packed_ref, 3, dot(mixed[...], delta_branch[...], 0, 0))
 
 
 def put_block(packed_ref, block, total):
@@ -349,55 +351,259 @@
         ].astype(jnp.bfloat16)
 
 
-def attention_half(
-    token_ref, mod_ref, rows_ref, grad_ref, packed_ref, small,
-    input_one, projected, soft, delta_residual, delta_mixed, delta_projected,
+def attention_latent(
+    latent, token_ref, mod_ref, rows_ref, grad_ref, small,
+    projected, soft, delta_residual, delta_mixed, delta_projected,
 ):
-    latents, positions, width = token_ref.shape
+    positions, width = token_ref.shape[1:]
     heads = width // HEAD
-
-    def one(latent, carry):
-        scale_one = mod_ref[latent, 1:2]
-        rows = pl.ds(pl.multiple_of(latent * positions, 16), positions)
-        for pair in range(heads // 2):
-            low = 2 * pair * HEAD
-            q2, k2, v2 = (
-                projected[rows, at * width + low : at * width + low + 2 * HEAD] for at in range(3)
+    scale_one = mod_ref[latent, 1:2]
+    rows = pl.ds(pl.multiple_of(latent * positions, 16), positions)
+    for pair in range(heads // 2):
+        low = 2 * pair * HEAD
+        q2, k2, v2 = (
+            projected[rows, at * width + low : at * width + low + 2 * HEAD] for at in range(3)
+        )
+        m2 = delta_mixed[rows, low : low + 2 * HEAD]
+        found = ([], [], [])
+        for at in range(2):
+            here = slice(at * HEAD, (at + 1) * HEAD)
+            weights = soft[latent * heads + 2 * pair + at]
+            delta_soft = dot(m2[:, here], v2[:, here], 1, 1)
+            inner = jnp.sum(delta_soft * weights, axis=-1, keepdims=True)
+            delta_scores = (weights * (delta_soft - inner)).astype(jnp.bfloat16)
+            found[0].append(dot(delta_scores, k2[:, here]) * HEAD ** (-0.5))
+            found[1].append(dot(delta_scores, q2[:, here], 0, 0) * HEAD ** (-0.5))
+            found[2].append(dot(weights.astype(jnp.bfloat16), m2[:, here], 0, 0))
+        for at in range(3):
+            delta_projected[rows, at * width + low : at * width + low + 2 * HEAD] = (
+                jnp.concatenate(found[at], axis=1).astype(jnp.bfloat16)
             )
-            m2 = delta_mixed[rows, low : low + 2 * HEAD]
-            found = ([], [], [])
-            for at in range(2):
-                here = slice(at * HEAD, (at + 1) * HEAD)
-                weights = soft[latent * heads + 2 * pair + at]
-                delta_soft = dot(m2[:, here], v2[:, here], 1, 1)
-                inner = jnp.sum(delta_soft * weights, axis=-1, keepdims=True)
-                delta_scores = (weights * (delta_soft - inner)).astype(jnp.bfloat16)
-                found[0].append(dot(delta_scores, k2[:, here]) * HEAD ** (-0.5))
-                found[1].append(dot(delta_scores, q2[:, here], 0, 0) * HEAD ** (-0.5))
-                found[2].append(dot(weights.astype(jnp.bfloat16), m2[:, here], 0, 0))
-            for at in range(3):
-                delta_projected[rows, at * width + low : at * width + low + 2 * HEAD] = (
-                    jnp.concatenate(found[at], axis=1).astype(jnp.bfloat16)
-                )
-        small[16:17] += column_sum(delta_projected[rows, :width].astype(jnp.float32))
-        small[17:18] += column_sum(delta_projected[rows, 2 * width :].astype(jnp.float32))
-        delta_input = dot(delta_projected[rows, :], rows_ref[:, : 3 * width], 1, 1)
-        normed_one, inv_one = normalize(token_ref[latent].astype(jnp.float32))
-        grad_ref[latent] = (
-            delta_residual[rows, :]
-            + norm_back(delta_input * (1.0 + scale_one), normed_one, inv_one)
-        ).astype(jnp.bfloat16)
-        small[pl.ds(latent * 6, 1)] = column_sum(delta_input)
-        small[pl.ds(latent * 6 + 1, 1)] = column_sum(delta_input * normed_one)
-        return carry
-
-    lax.fori_loop(0, latents, one, 0)
+    small[16:17] += column_sum(delta_projected[rows, :width].astype(jnp.float32))
+    small[17:18] += column_sum(delta_projected[rows, 2 * width :].astype(jnp.float32))
+    delta_input = dot(delta_projected[rows, :], rows_ref[:, : 3 * width], 1, 1)
+    normed_one, inv_one = normalize(token_ref[latent].astype(jnp.float32))
+    grad_ref[latent] = (
+        delta_residual[rows, :]
+        + norm_back(delta_input * (1.0 + scale_one), normed_one, inv_one)
+    ).astype(jnp.bfloat16)
+    small[pl.ds(latent * 6, 1)] = column_sum(delta_input)
+    small[pl.ds(latent * 6 + 1, 1)] = column_sum(delta_input * normed_one)
+
+
+def attention_grads(packed_ref, input_one, delta_projected):
+    width = input_one.shape[1]
     for block in range(3):
         put_block(
             packed_ref,
             block,
             dot(input_one[...], delta_projected[:, block * width : (block + 1) * width], 0, 0),
         )
+
+
+def fused_kernel(
+    token_ref, upstream_ref, mod_ref, bias_ref, rows_ref, down_ref, silu_ref, cond_ref,
+    out_ref, grad_ref, sum_out, small_out, silu_out,
+    small, input_one, projected, soft, mixed, input_two, active, delta_hidden, delta_feed,
+    delta_branch, delta_residual, delta_mixed, delta_projected,
+    packed_ref, small_low, core_in, core_sum, across_in, across_sum, beside_in, beside_sum,
+    line_in, silu_part, send_sem, recv_sem,
+):
+    s, r = lax.axis_index("shard"), lax.axis_index("replica")
+    x, z = lax.rem(r, 2), r // 2
+    c, y = lax.rem(s, 2), s // 2
+    core, across, corner = (flip(s), r), (lax.rem(s + 2, 4), r), (flip(lax.rem(s + 2, 4)), r)
+    beside = (s, flip(r))
+    line_z = [lax.rem(z + step, 4) for step in (1, 2, 3)]
+    line = [(s, 2 * at + x) for at in line_z]
+    meet([core, across, corner, beside] + line)
+    copies = Copies(send_sem, recv_sem)
+    split, whole, width = 4 * 96, packed_ref.shape[1], packed_ref.shape[2]
+    parts = [(split, whole - split, 128 * at, 128) for at in range(3)] + [(0, split, 0, width)]
+
+    def span(first, count):
+        return pl.ds(pl.multiple_of(first, 16), count)
+
+    def add_rows(count, body):
+        def one(step, carry):
+            body(step * 96)
+            return carry
+
+        lax.fori_loop(0, count // 96, one, 0)
+
+    def f32(value):
+        return value.astype(jnp.float32)
+
+    made = {}
+
+    def start_core(part):
+        first, count, left, columns = parts[part]
+        rows, cols = pl.ds(first, count), pl.ds(left, columns)
+        made["core", part] = [
+            copies.start(
+                packed_ref.at[2 * side + 1 - c, rows, cols], core_in.at[side, rows, cols], core
+            )
+            for side in (1 - y, y)
+        ]
+
+    def stage_across(part):
+        first, count, left, columns = parts[part]
+        cols = pl.ds(left, columns)
+        for at, side in enumerate((1 - y, y)):
+            made["core", part][at].wait_recv()
+
+            def add(low, side=side):
+                rows = span(first + low, 96)
+                core_sum[side, rows, cols] = (
+                    f32(packed_ref[2 * side + c, rows, cols]) + f32(core_in[side, rows, cols])
+                ).astype(jnp.bfloat16)
+
+            add_rows(count, add)
+            if at == 0:
+                rows = pl.ds(first, count)
+                made["across", part] = copies.start(
+                    core_sum.at[side, rows, cols], across_in.at[rows, cols], across
+                )
+
+    def stage_beside(part):
+        first, count, left, columns = parts[part]
+        cols, half = pl.ds(left, columns), count // 2
+        made["across", part].wait_recv()
+
+        def add(low):
+            rows = span(first + low, 96)
+            across_sum[rows, cols] = (
+                f32(core_sum[y, rows, cols]) + f32(across_in[rows, cols])
+            ).astype(jnp.bfloat16)
+
+        add_rows(count, add)
+        made["beside", part] = copies.start(
+            across_sum.at[span(first + (1 - x) * half, half), cols],
+            beside_in.at[pl.ds(first, half), cols],
+            beside,
+        )
+
+    def stage_line(part):
+        first, count, left, columns = parts[part]
+        cols, half, share = pl.ds(left, columns), count // 2, count // 8
+        made["beside", part].wait_recv()
+
+        def add(low):
+            rows = span(first + low, 96)
+            beside_sum[rows, cols] = (
+                f32(across_sum[span(first + x * half + low, 96), cols])
+                + f32(beside_in[rows, cols])
+            ).astype(jnp.bfloat16)
+
+        add_rows(half, add)
+        made["line", part] = [
+            copies.start(
+                beside_sum.at[span(first + line_z[at] * share, share), cols],
+                line_in.at[at, pl.ds(first, share), cols],
+                line[at],
+            )
+            for at in range(3)
+        ]
+
+    def stage_gather(part):
+        first, count, left, columns = parts[part]
+        cols, half, share = pl.ds(left, columns), count // 2, count // 8
+        for copy in made["line", part]:
+            copy.wait_recv()
+        total = f32(beside_sum[span(first + z * share, share), cols])
+        for at in range(3):
+            total = total + f32(line_in[at, pl.ds(first, share), cols])
+        rows = span(first + x * half + z * share, share)
+        sum_out[rows, cols] = total.astype(jnp.bfloat16)
+        own = sum_out.at[rows, cols]
+        made["gather", part] = [copies.start(own, own, peer) for peer in line]
+        made["last", part] = [copies.start(own, own, beside)]
+
+    def stage_last(part):
+        first, count, left, columns = parts[part]
+        cols, half, share = pl.ds(left, columns), count // 2, count // 8
+        for at in range(3):
+            made["gather", part][at].wait_recv()
+            origin = lax.rem(z + 3 - at, 4)
+            piece = sum_out.at[span(first + x * half + origin * share, share), cols]
+            made["last", part].append(copies.start(piece, piece, beside))
+
+    def attention(latent):
+        attention_latent(
+            latent, token_ref, mod_ref, rows_ref, grad_ref, small,
+            projected, soft, delta_residual, delta_mixed, delta_projected,
+        )
+
+    small[...] = jnp.zeros_like(small)
+    small[12:14] = silu_ref[...].astype(jnp.float32)
+    feed_half(
+        token_ref, upstream_ref, mod_ref, bias_ref, rows_ref, down_ref,
+        out_ref, packed_ref, small,
+        input_one, projected, soft, mixed, input_two, active, delta_hidden, delta_feed,
+        delta_branch, delta_residual, delta_mixed,
+    )
+    for part in range(3):
+        start_core(part)
+    put_block(packed_ref, 3, dot(mixed[...], delta_branch[...], 0, 0))
+    for part in range(3):
+        stage_across(part)
+    attention(0)
+    stage_beside(0)
+    attention(1)
+    stage_beside(1)
+    stage_line(0)
+    small_low[...] = small[...].astype(jnp.bfloat16)
+    small_out[s, x, z] = small_low[...]
+    small_line = [copies.start(small_low, small_out.at[s, x, z], peer) for peer in line]
+    attention_grads(packed_ref, input_one, delta_projected)
+    start_core(3)
+    stage_beside(2)
+    stage_line(1)
+    stage_across(3)
+    for copy in small_line:
+        copy.wait_recv()
+    small_beside = copies.start(small_out.at[s, x], small_out.at[s, x], beside)
+    stage_gather(0)
+    stage_line(2)
+    small_beside.wait_recv()
+    small_across = copies.start(small_out.at[s], small_out.at[s], across)
+    stage_gather(1)
+    stage_last(0)
+    stage_beside(3)
+    stage_gather(2)
+    stage_last(1)
+    stage_line(3)
+    small_across.wait_recv()
+    far = across[0]
+    small_core = [
+        copies.start(small_out.at[s], small_out.at[s], core),
+        copies.start(small_out.at[far], small_out.at[far], core),
+    ]
+    stage_last(2)
+    for copy in small_core:
+        copy.wait_recv()
+    depth = cond_ref.shape[0]
+    left = jnp.concatenate([small_out[at, x, z, 0:16] for at in range(4)], axis=0)
+    row = lax.rem(lax.rem(lax.broadcasted_iota(jnp.int32, left.shape, 0), 16), 6)
+    total = jnp.zeros((64, depth), jnp.float32)
+    for block in range(6):
+        chosen = jnp.where(row == block, left, jnp.zeros_like(left))
+        total = total + dot(chosen, cond_ref[:, block * width : (block + 1) * width], 1, 1)
+    silu_part[...] = jnp.zeros_like(silu_part)
+    silu_part[:, :, 0:depth] = total.reshape(4, 16, depth)
+    silu_out[s] = silu_part[s]
+    silu_copies = [
+        copies.start(silu_part.at[peer[0]], silu_out.at[s], peer)
+        for peer in (across, corner, core)
+    ]
+    stage_gather(3)
+    stage_last(3)
+    for copy in silu_copies:
+        copy.wait_recv()
+    for part in range(4):
+        for copy in made["last", part]:
+            copy.wait_recv()
+    copies.finish()
 
 
 def block_kernel(
@@ -414,10 +620,13 @@
         input_one, projected, soft, mixed, input_two, active, delta_hidden, delta_feed,
         delta_branch, delta_residual, delta_mixed,
     )
-    attention_half(
-        token_ref, mod_ref, rows_ref, grad_ref, packed_ref, small,
-        input_one, projected, soft, delta_residual, delta_mixed, delta_projected,
-    )
+    put_block(packed_ref, 3, dot(mixed[...], delta_branch[...], 0, 0))
+    for latent in range(token_ref.shape[0]):
+        attention_latent(
+            latent, token_ref, mod_ref, rows_ref, grad_ref, small,
+            projected, soft, delta_residual, delta_mixed, delta_projected,
+        )
+    attention_grads(packed_ref, input_one, delta_projected)
     small_ref[...] = small[...].astype(jnp.bfloat16)
 
 
@@ -457,253 +666,90 @@
     )(tokens, cotangent, modulation, biases, rows_full, down_full, silu_cond)
 
 
-def reduce_kernel(
-    packed_ref,
-    small_ref,
-    cond_ref,
-    sum_out,
-    small_out,
-    silu_out,
-    core_in,
-    core_sum,
-    across_in,
-    across_sum,
-    beside_in,
-    beside_sum,
-    line_in,
-    silu_part,
-    send_sem,
-    recv_sem,
-):
-    s, r = lax.axis_index("shard"), lax.axis_index("replica")
-    x, z = lax.rem(r, 2), r // 2
-    c, y = lax.rem(s, 2), s // 2
-    core, across, corner = (flip(s), r), (lax.rem(s + 2, 4), r), (flip(lax.rem(s + 2, 4)), r)
-    beside = (s, flip(r))
-    line_z = [lax.rem(z + step, 4) for step in (1, 2, 3)]
-    line = [(s, 2 * at + x) for at in line_z]
-    meet([core, across, corner, beside] + line)
-    copies = Copies(send_sem, recv_sem)
-    parts = range(3)
-    cols = [pl.ds(128 * part, 128) for part in parts]
-    whole = packed_ref.shape[1]
-    half, share = whole // 2, whole // 8
-
-    def add_rows(count, body):
-        def one(step, carry):
-            body(pl.multiple_of(step * ROW_STEP, 16))
-            return carry
-
-        lax.fori_loop(0, count // ROW_STEP, one, 0)
-
-    def f32(value):
-        return value.astype(jnp.float32)
-
-    core_copies = []
-    for part in parts:
-        core_copies.append(
-            [
-                copies.start(
-                    packed_ref.at[2 * side + 1 - c, :, cols[part]],
-                    core_in.at[side, :, cols[part]],
-                    core,
-                )
-                for side in (1 - y, y)
-            ]
-        )
-    small_out[s, x, z] = small_ref[...]
-    own_small = small_out.at[s, x, z]
-    small_line = [copies.start(own_small, own_small, peer) for peer in line]
-
-    across_copies = []
-    for part in parts:
-        for at, side in enumerate((1 - y, y)):
-            core_copies[part][at].wait_recv()
-
-            def add(low, part=part, side=side):
-                rows = pl.ds(low, ROW_STEP)
-                core_sum[side, rows, cols[part]] = (
-                    f32(packed_ref[2 * side + c, rows, cols[part]])
-                    + f32(core_in[side, rows, cols[part]])
-                ).astype(jnp.bfloat16)
-
-            add_rows(whole, add)
-            if at == 0:
-                across_copies.append(
-                    copies.start(
-                        core_sum.at[side, :, cols[part]], across_in.at[:, cols[part]], across
-                    )
-                )
-
-    for copy in small_line:
-        copy.wait_recv()
-    small_beside = copies.start(small_out.at[s, x], small_out.at[s, x], beside)
-
-    beside_copies, line_copies, gather_copies, last_copies = {}, {}, {}, {}
-
-    def stage_beside(part):
-        across_copies[part].wait_recv()
-
-        def add(low):
-            rows = pl.ds(low, ROW_STEP)
-            across_sum[rows, cols[part]] = (
-                f32(core_sum[y, rows, cols[part]]) + f32(across_in[rows, cols[part]])
-            ).astype(jnp.bfloat16)
-
-        add_rows(whole, add)
-        beside_copies[part] = copies.start(
-            across_sum.at[pl.ds(pl.multiple_of((1 - x) * half, 16), half), cols[part]],
-            beside_in.at[:, cols[part]],
-            beside,
-        )
-
-    def stage_line(part):
-        beside_copies[part].wait_recv()
-
-        def add(low):
-            rows = pl.ds(low, ROW_STEP)
-            from_rows = pl.ds(pl.multiple_of(x * half + low, 16), ROW_STEP)
-            beside_sum[rows, cols[part]] = (
-                f32(across_sum[from_rows, cols[part]]) + f32(beside_in[rows, cols[part]])
-            ).astype(jnp.bfloat16)
-
-        add_rows(half, add)
-        line_copies[part] = [
-            copies.start(
-                beside_sum.at[pl.ds(pl.multiple_of(line_z[at] * share, 16), share), cols[part]],
-                line_in.at[at, :, cols[part]],
-                line[at],
-            )
-            for at in range(3)
-        ]
-
-    def stage_gather(part):
-        for copy in line_copies[part]:
-            copy.wait_recv()
-        rows = pl.ds(pl.multiple_of(z * share, 16), share)
-        total = f32(beside_sum[rows, cols[part]])
-        for at in range(3):
-            total = total + f32(line_in[at, :, cols[part]])
-        sum_out[x, z, :, cols[part]] = total.astype(jnp.bfloat16)
-        own = sum_out.at[x, z, :, cols[part]]
-        gather_copies[part] = [copies.start(own, own, peer) for peer in line]
-        last_copies[part] = [copies.start(own, own, beside)]
-
-    def stage_last(part):
-        for at in range(3):
-            gather_copies[part][at].wait_recv()
-            origin = lax.rem(z + 3 - at, 4)
-            piece = sum_out.at[x, origin, :, cols[part]]
-            last_copies[part].append(copies.start(piece, piece, beside))
-
-    stage_beside(0)
-    small_beside.wait_recv()
-    small_across = copies.start(small_out.at[s], small_out.at[s], across)
-    stage_beside(1)
-    stage_line(0)
-    stage_beside(2)
-    stage_line(1)
-    stage_gather(0)
-    small_across.wait_recv()
-    far = across[0]
-    small_core = [
-        copies.start(small_out.at[s], small_out.at[s], core),
-        copies.start(small_out.at[far], small_out.at[far], core),
-    ]
-    stage_line(2)
-    stage_gather(1)
-    stage_last(0)
-
-    for copy in small_core:
-        copy.wait_recv()
-    depth = cond_ref.shape[0]
-    width = packed_ref.shape[-1]
-    left = jnp.concatenate([small_out[at, x, z, 0:16] for at in range(4)], axis=0)
-    row = lax.rem(lax.rem(lax.broadcasted_iota(jnp.int32, left.shape, 0), 16), 6)
-    total = jnp.zeros((64, depth), jnp.float32)
-    for block in range(6):
-        chosen = jnp.where(row == block, left, jnp.zeros_like(left))
-        total = total + lax.dot_general(
-            chosen,
-            cond_ref[:, block * width : (block + 1) * width],
-            (((1,), (1,)), ((), ())),
-            preferred_element_type=jnp.float32,
-        )
-    silu_part[...] = jnp.zeros_like(silu_part)
-    silu_part[:, :, 0:depth] = total.reshape(4, 16, depth)
-    silu_out[s] = silu_part[s]
-    silu_copies = [
-        copies.start(silu_part.at[peer[0]], silu_out.at[s], peer)
-        for peer in (across, corner, core)
-    ]
-    stage_gather(2)
-    stage_last(1)
-    stage_last(2)
-    for copy in silu_copies:
-        copy.wait_recv()
-    for part in parts:
-        for copy in last_copies[part]:
-            copy.wait_recv()
-    copies.finish()
-
-
 def reduce_gradients(
-    packed, small, w_rows, latents, shards, replicas
+    packed, small, w_rows, latents
 ):
     width = packed.shape[-1]
     own_rows, six_width = w_rows.shape[0], 6 * width
     delta_modulation = small[: 6 * latents].reshape(latents, six_width)
     silu_cond = small[6 * latents : 7 * latents]
     bias_local = small[16:24].astype(jnp.float32).reshape(-1)
-    if shards != 4 or replicas != 8 or latents != 2:
-        summed = lax.psum_scatter(
-            packed.reshape(-1, width).astype(jnp.float32), "shard", scatter_dimension=0, tiled=True
-        )
-        summed = lax.psum(summed, "replica")
-        axes = ("shard", "replica")
-        cond_matrix = lax.all_gather(w_rows[:, :six_width], "shard", axis=0, tiled=True)
-        return (
-            summed,
-            lax.all_gather(delta_modulation, axes, axis=0, tiled=True),
-            lax.all_gather(silu_cond, axes, axis=0, tiled=True),
-            lax.psum(bias_local, axes),
-            matrix_multiply("le,de->ld", delta_modulation, cond_matrix),
-        )
-    whole = packed.shape[1]
+    summed = lax.psum_scatter(
+        packed.reshape(-1, width).astype(jnp.float32), "shard", scatter_dimension=0, tiled=True
+    )
+    summed = lax.psum(summed, "replica")
+    axes = ("shard", "replica")
+    cond_matrix = lax.all_gather(w_rows[:, :six_width], "shard", axis=0, tiled=True)
+    return (
+        summed,
+        lax.all_gather(delta_modulation, axes, axis=0, tiled=True),
+        lax.all_gather(silu_cond, axes, axis=0, tiled=True),
+        lax.psum(bias_local, axes),
+        matrix_multiply("le,de->ld", delta_modulation, cond_matrix),
+    )
+
+
+def fused_gradients(
+    tokens, cotangent, modulation, biases, rows_full, down_full, silu_cond, w_rows,
+    shards, replicas,
+):
+    latents, positions, width = tokens.shape
+    count, hidden_width = latents * positions, down_full.shape[0]
+    own_rows, six_width = w_rows.shape[0], 6 * width
+    whole = 8 * own_rows + hidden_width // 4
+    bf16, f32 = jnp.bfloat16, jnp.float32
     vmem = pl.BlockSpec(memory_space=pltpu.VMEM)
-    bf16 = jnp.bfloat16
-    summed, every, silu_parts = pl.pallas_call(
-        reduce_kernel,
+    block_out, tokens_grad, summed, every, silu_parts = pl.pallas_call(
+        fused_kernel,
         out_shape=(
-            jax.ShapeDtypeStruct((2, 4, whole // 8, width), bf16),
+            jax.ShapeDtypeStruct(tokens.shape, bf16),
+            jax.ShapeDtypeStruct(tokens.shape, bf16),
+            jax.ShapeDtypeStruct((whole, width), bf16),
             jax.ShapeDtypeStruct((shards, 2, 4, 32, width), bf16),
-            jax.ShapeDtypeStruct((shards, 16, 128), jnp.float32),
+            jax.ShapeDtypeStruct((shards, 16, 128), f32),
         ),
-        in_specs=[vmem] * 3,
-        out_specs=(vmem,) * 3,
+        in_specs=[vmem] * 8,
+        out_specs=(vmem,) * 5,
         scratch_shapes=[
+            pltpu.VMEM((32, width), f32),
+            pltpu.VMEM((count, width), bf16),
+            pltpu.VMEM((count, 3 * width), bf16),
+            pltpu.VMEM((latents * HEADS, positions, positions), f32),
+            pltpu.VMEM((count, width), bf16),
+            pltpu.VMEM((count, width), bf16),
+            pltpu.VMEM((count, hidden_width), bf16),
+            pltpu.VMEM((count, hidden_width), bf16),
+            pltpu.VMEM((count, width), bf16),
+            pltpu.VMEM((count, width), bf16),
+            pltpu.VMEM((count, width), f32),
+            pltpu.VMEM((count, width), bf16),
+            pltpu.VMEM((count, 3 * width), bf16),
+            pltpu.VMEM((shards, whole, width), bf16),
+            pltpu.VMEM((32, width), bf16),
             pltpu.VMEM((2, whole, width), bf16),
             pltpu.VMEM((2, whole, width), bf16),
             pltpu.VMEM((whole, width), bf16),
             pltpu.VMEM((whole, width), bf16),
-            pltpu.VMEM((whole // 2, width), bf16),
-            pltpu.VMEM((whole // 2, width), bf16),
-            pltpu.VMEM((3, whole // 8, width), bf16),
-            pltpu.VMEM((shards, 16, 128), jnp.float32),
-            pltpu.SemaphoreType.DMA((64,)),
-            pltpu.SemaphoreType.DMA((64,)),
+            pltpu.VMEM((whole, width), bf16),
+            pltpu.VMEM((whole, width), bf16),
+            pltpu.VMEM((3, whole, width), bf16),
+            pltpu.VMEM((shards, 16, 128), f32),
+            pltpu.SemaphoreType.DMA((96,)),
+            pltpu.SemaphoreType.DMA((96,)),
         ],
         compiler_params=pltpu.CompilerParams(
             collective_id=1, has_side_effects=True, vmem_limit_bytes=VMEM_BYTES
         ),
-        name="reduce_gradients",
-    )(packed, small, w_rows[:, :six_width])
+        name="fused_gradients",
+    )(tokens, cotangent, modulation, biases, rows_full, down_full, silu_cond, w_rows)
     every = every.transpose(0, 2, 1, 3, 4).reshape(shards * replicas, 32, width)
-    bias_rows = every[:, 16 : 16 + bias_local.shape[0] // width]
+    bias_rows = every[:, 16 : 16 + 8]
     delta_silu = silu_parts[:, : 6 * latents, :own_rows]
     delta_silu = delta_silu.reshape(shards, latents, 6, own_rows).sum(axis=2)
     return (
-        summed.reshape(whole, width),
+        block_out,
+        tokens_grad,
+        summed,
         every[:, : 6 * latents].reshape(-1, six_width),
         every[:, 6 * latents : 7 * latents].reshape(-1, width),
         bias_rows.astype(jnp.float32).sum(axis=0).reshape(-1),
@@ -739,7 +785,7 @@
     modulation = jnp.pad(
         modulation.reshape(latents, 6, embedding_width), ((0, 0), (0, 2), (0, 0))
     )
-    block_out, tokens_grad, packed, small = block_gradients(
+    arguments = (
         tokens,
         cotangent,
         modulation,
@@ -748,9 +794,12 @@
         shrink_weight,
         silu_cond,
     )
-    summed, every_modulation, every_silu, bias_rest, delta_silu = reduce_gradients(
-        packed, small, w_rows, latents, shards, replicas
-    )
+    if shards != 4 or replicas != 8 or latents != 2:
+        block_out, tokens_grad, packed, small = block_gradients(*arguments)
+        reduced = reduce_gradients(packed, small, w_rows, latents)
+    else:
+        block_out, tokens_grad, *reduced = fused_gradients(*arguments, w_rows, shards, replicas)
+    summed, every_modulation, every_silu, bias_rest, delta_silu = reduced
     blocks = rows_full.shape[1] // embedding_width
     shard_rows = w_rows.shape[0]
     shard_at = lax.axis_index("shard")

time: 122 us -> 110 us (0.902)
  Pallas kernels: 102 us -> 89.7 us
  local copies, waits for them, and re-layouts: 11.4 us -> 9.84 us
    pallas_call x3 -> x2, Pallas kernels: 102 us -> 89.7 us  [the longest x1 65.7 us: fused_gradients(): pl.pallas_call(fused_kernel, out_shape=(jax.ShapeDtypeStruct(tokens.shape...]
    slice x5 -> x3, local copies, waits for them, and re-layouts: 3.83 us -> 0.87 us  [the longest x1 0.77 us: fused_gradients(): delta_silu = silu_parts[:, :6 * latents, :own_rows]]
    unnamed x27 -> x31, local copies, waits for them, and re-layouts: 2.4 us -> 3.18 us
where the time goes in v3:
time: 110 us
  Pallas kernels  89.7 us (82%)
  local copies, waits for them, and re-layouts  9.84 us (9%)
  other arithmetic  8.71 us (8%)
    pallas_call x1, Pallas kernels, fused_gradients(): pl.pallas_call(fused_kernel, out_shape=(jax.ShapeDtypeStruct(tokens.shape...  65.7 us
    pallas_call x1, Pallas kernels, gather_weights(): pl.pallas_call(gather_kernel, out_shape=(jax.ShapeDtypeStruct((shards, ow...  24 us
    sub x3, other arithmetic, adam_step(): master - learn_rate * (first_hat / (jnp.sqrt(second_hat) + adam_eps) + we...  7.21 us
    unnamed x31, local copies, waits for them, and re-layouts  3.18 us

profile of v3, /device:TPU:0, one launch (start us, length us, event | category | flops | bytes accessed | tf_op | source)
XLA Modules:
  0.0 109.5 jit_solution(15174786654635316311)
XLA Ops:
  0.6 0.7 fusion.16.silu_ref
  1.4 0.1 reshape.86
  1.4 1.3 %pad_bitcast_fusion.bias_ref = bf16[16,128]{1,0:T(8,128)(2,1)} fusion(bf16[1344]{0:T(1024)(128)(2,1)} %param.17), kind=kLoop, calls=%fused_computation.38 | loop fusion | bytes 6784 | tf_op jit(solution)/shard_map/reshape | solution.py:210
  2.7 0.6 pad.13.silu_ref
  3.4 24.0 %gather_weights.1 = (bf16[4,96,3072]{2,1,0:T(8,128)(2,1)}, bf16[4,384,384]{2,1,0:T(8,128)(2,1)}, bf16[4,16,128]{2,1,0:T(8,128)(2,1)}, f32[16,384]{1,0:T(8,128)}) custom-call(bf16[96,5376]{1,0:T(8,128)(2,1)} %cond_ref.1, bf16[384,384]{1,0:T(8,128)(2,1)} %down_ref.1, bf16[16,128]{1,0:T(8,128)(2,1)} %pad_bitcast_fusion.bias_ref, bf16[4,16,128]{2,1,0:T(8,128)(2,1)} %pad.13.silu_ref), custom_call_target="tpu_custom_call" | custom-call | tf_op jit(solution)/shard_map/gather_weights/pallas_call | solution.py:213
  27.4 0.7 reshape.88
  28.1 0.7 copy.33
  28.9 0.1 reshape.98
  29.0 0.6 slice.44.bias_ref
  29.6 0.6 pad.14.mod_ref
  30.2 65.7 %fused_gradients.1 = (bf16[2,256,384]{2,1,0:T(8,128)(2,1)}, bf16[2,256,384]{2,1,0:T(8,128)(2,1)}, bf16[1152,384]{1,0:T(8,128)(2,1)}, bf16[4,2,4,32,384]{4,3,2,1,0:T(8,128)(2,1)}, f32[4,16,128]{2,1,0:T(8,128)}) custom-call(bf16[2,256,384]{2,1,0:T(8,128)(2,1)} %token_ref.1, bf16[2,256,384]{2,1,0:T(8,128)(2,1)} %upstream_ref.1, f32[2,8,384]{2,1,0:T(8,128)} %pad.14.mod_ref, ...), custom_call_target="tpu_custom_call" | custom-call | tf_op jit(solution)/shard_map/fused_gradients/pallas_call | solution.py:702
  95.9 0.8 copy.27
  96.7 0.6 fusion.18
  97.3 1.1 %slice.39 = bf16[768,384]{1,0:T(8,128)(2,1)S(1)} slice(bf16[1152,384]{1,0:T(8,128)(2,1)} %get-tuple-element.29), slice={[0:768], [0:384]} | slice | bytes 1179648 | tf_op jit(solution)/shard_map/slice | solution.py:812
  98.6 0.1 copy.30
  98.7 0.9 copy-done.4
  99.6 0.1 copy.28
  99.9 0.3 reshape.96
  100.4 0.7 convert_subtract_fusion.2
  101.1 0.4 fusion.7
  101.5 2.7 %convert_subtract_fusion.1 = (f32[384,384]{1,0:T(8,128)}, f32[384,384]{1,0:T(8,128)}, f32[384,384]{1,0:T(8,128)}) fusion(bf16[384,384]{1,0:T(8,128)(2,1)S(1)} %copy-done.1, bf16[1152,384]{1,0:T(8,128)(2,1)} %get-tuple-element.29, bf16[384,384]{1,0:T(8,128)(2,1)S(1)} %copy-done.7, bf16[384,384]{1,0:T(8,128)(2,1)S(1)} %copy-done.8), kind=kLoop, calls=%fused_computation.11 | loop fusion | flops 2801664 | bytes 2949120 | tf_op jit(solution)/shard_map/sub | solution.py:50
  104.2 3.8 %convert_subtract_fusion = (f32[96,5376]{1,0:T(8,128)}, f32[96,5376]{1,0:T(8,128)}, f32[96,5376]{1,0:T(8,128)}) fusion(bf16[96,5376]{1,0:T(8,128)(2,1)S(1)} %copy-done, f32[96,3072]{1,0:T(8,128)S(1)} %bitcast.23, f32[96,2304]{1,0:T(8,128)S(1)} %fusion.7, bf16[96,5376]{1,0:T(8,128)(2,1)S(1)} %copy-done.2, bf16[96,5376]{1,0:T(8,128)(2,1)S(1)} %copy-done.3), kind=kLoop, calls=%fused_computation.1 | loop fusion | flops 9805824 | bytes 11354112 | tf_op jit(solution)/shard_map/sub | solution.py:50
  108.0 0.7 copy.36
  108.8 0.7 copy.37
  (41 shorter events, 0.5 us)
Async XLA Ops:
  1.3 28.8 %copy-start.10 = (bf16[2,384]{1,0:T(2,128)(2,1)}, bf16[2,384]{1,0:T(2,128)(2,1)S(1)}, u32[]{:S(2)}) copy-start(bf16[2,384]{1,0:T(2,128)(2,1)S(1)} %fusion.16.silu_ref) | copy-start | bytes 4612
  30.2 66.5 %copy-start.11 = (bf16[2,384]{1,0:T(2,128)(2,1)S(1)}, bf16[2,384]{1,0:T(2,128)(2,1)}, u32[]{:S(2)}) copy-start(bf16[2,384]{1,0:T(2,128)(2,1)} %param.13) | copy-start | bytes 4612
  98.5 1.1 %copy-start.4 = (bf16[4,2,4,32,384]{4,3,2,1,0:T(8,128)(2,1)S(1)}, bf16[4,2,4,32,384]{4,3,2,1,0:T(8,128)(2,1)}, u32[]{:S(2)}) copy-start(bf16[4,2,4,32,384]{4,3,2,1,0:T(8,128)(2,1)} %get-tuple-element.28) | copy-start | bytes 2359300
  98.7 1.7 %copy-start.9 = (bf16[1344]{0:T(1024)(128)(2,1)S(1)}, bf16[1344]{0:T(1024)(128)(2,1)}, u32[]{:S(2)}) copy-start(bf16[1344]{0:T(1024)(128)(2,1)} %param.17) | copy-start | bytes 8068
  98.7 1.7 %copy-start.12 = (bf16[1344]{0:T(1024)(128)(2,1)S(1)}, bf16[1344]{0:T(1024)(128)(2,1)}, u32[]{:S(2)}) copy-start(bf16[1344]{0:T(1024)(128)(2,1)} %param.22) | copy-start | bytes 8068
  98.7 1.7 %copy-start.13 = (bf16[1344]{0:T(1024)(128)(2,1)S(1)}, bf16[1344]{0:T(1024)(128)(2,1)}, u32[]{:S(2)}) copy-start(bf16[1344]{0:T(1024)(128)(2,1)} %param.23) | copy-start | bytes 8068
  99.7 1.8 %copy-start.1 = (bf16[384,384]{1,0:T(8,128)(2,1)S(1)}, bf16[384,384]{1,0:T(8,128)(2,1)}, u32[]{:S(2)}) copy-start(bf16[384,384]{1,0:T(8,128)(2,1)} %down_ref.1) | copy-start | bytes 884740
  99.7 1.7 %copy-start.7 = (bf16[384,384]{1,0:T(8,128)(2,1)S(1)}, bf16[384,384]{1,0:T(8,128)(2,1)}, u32[]{:S(2)}) copy-start(bf16[384,384]{1,0:T(8,128)(2,1)} %param.20) | copy-start | bytes 884740
  99.7 1.7 %copy-start.8 = (bf16[384,384]{1,0:T(8,128)(2,1)S(1)}, bf16[384,384]{1,0:T(8,128)(2,1)}, u32[]{:S(2)}) copy-start(bf16[384,384]{1,0:T(8,128)(2,1)} %param.21) | copy-start | bytes 884740
  101.1 3.1 %copy-start = (bf16[96,5376]{1,0:T(8,128)(2,1)S(1)}, bf16[96,5376]{1,0:T(8,128)(2,1)}, u32[]{:S(2)}) copy-start(bf16[96,5376]{1,0:T(8,128)(2,1)} %cond_ref.1) | copy-start | bytes 3096580
  101.1 3.1 %copy-start.2 = (bf16[96,5376]{1,0:T(8,128)(2,1)S(1)}, bf16[96,5376]{1,0:T(8,128)(2,1)}, u32[]{:S(2)}) copy-start(bf16[96,5376]{1,0:T(8,128)(2,1)} %param.18) | copy-start | bytes 3096580
  101.1 3.1 %copy-start.3 = (bf16[96,5376]{1,0:T(8,128)(2,1)S(1)}, bf16[96,5376]{1,0:T(8,128)(2,1)}, u32[]{:S(2)}) copy-start(bf16[96,5376]{1,0:T(8,128)(2,1)} %param.19) | copy-start | bytes 3096580
  104.2 3.8 %copy-start.6 = (bf16[2,256,384]{2,1,0:T(8,128)(2,1)S(1)}, bf16[2,256,384]{2,1,0:T(8,128)(2,1)}, u32[]{:S(2)}) copy-start(bf16[2,256,384]{2,1,0:T(8,128)(2,1)} %get-tuple-element.51) | copy-start | bytes 1179652
  104.2 4.5 %copy-start.5 = (bf16[2,256,384]{2,1,0:T(8,128)(2,1)S(1)}, bf16[2,256,384]{2,1,0:T(8,128)(2,1)}, u32[]{:S(2)}) copy-start(bf16[2,256,384]{2,1,0:T(8,128)(2,1)} %get-tuple-element.52) | copy-start | bytes 1179652
